TPU v7x, 32 devices: a whole 2x2x4 slice. The times are simulated.
32 devices in a mesh: tm: 8 (over z, x), seq: 2 (over y), mp: 2 (over core).
Axes of the slice: x: 2, y: 2, z: 4, core: 2. Of those that a mesh axis runs over, the one named last changes fastest.
Arguments:
- student_q: bfloat16 [2, 1024, 5120], P('seq', 'tm', 'mp'), may hold values from -110 to 110
- student_k: bfloat16 [2, 1024, 5120], P('seq', 'tm', 'mp'), may hold values from -6 to 6
- student_v: bfloat16 [2, 1024, 5120], P('seq', 'tm', 'mp'), may hold values from -6 to 6
- teacher_q: bfloat16 [2, 1024, 5120], P('seq', 'tm', 'mp'), may hold values from -110 to 110
- teacher_k: bfloat16 [2, 1024, 5120], P('seq', 'tm', 'mp'), may hold values from -6 to 6
- stagger: int32 [2], P('seq'), may hold values from 0 to 4, as said below
- clip_lengths: int32 [2, 3], P('seq'), may hold values from 1 to 5, 8 in all within a row
Outputs:
- generated: bfloat16 [2, 1024, 5120], P('seq', 'tm', 'mp')
- score_rows: bfloat16 [2, 1024, 5120], P('seq', 'tm', 'mp')
Inputs may be any that keep to these rules, and one draw needn't show every extreme that they name: `clip_lengths`: the lengths of each video sum to 8, and some clip has 5 blocks. `stagger`: some video has the value 8 // 2.
All inputs are finite; a program needn't handle non-finite values.
Results may differ from a plain program's by a relative error of at most 0.007.
Values may be sent and summed in bfloat16 or wider, within the bound.
No kernel may reach another device: no remote copies, remote signals or barrier semaphores. Data moves between devices by JAX's collectives and lax.ppermute only.
A program may use at most 64 MiB of HBM per device.

v0:
```python
import functools
import math

import jax
import jax.numpy as jnp
from jax import lax
from jax.experimental import pallas as pl
from jax.experimental.pallas import tpu as pltpu
from jax.sharding import PartitionSpec as P

HD = 128
TOK = 128
NEG = -1e30
RATE = math.log2(math.e) / math.sqrt(HD)
MIB = 2**20
VMEM = pl.BlockSpec(memory_space=pltpu.VMEM)
SMEM = pl.BlockSpec(memory_space=pltpu.SMEM)
WHOLE = pltpu.CompilerParams(vmem_limit_bytes=60 * MIB)
LOCAL = pltpu.CompilerParams(vmem_limit_bytes=24 * MIB)


def attend(q, k, v, bias):
    g = q.shape[0]
    scores = lax.dot_general(
        q.reshape(g * TOK, HD), k, (((1,), (1,)), ((), ())), preferred_element_type=jnp.float32
    )
    scores = scores.reshape(g, TOK, -1)
    if bias is not None:
        scores = scores + bias
    top = jnp.max(scores, axis=-1, keepdims=True)
    weights = jnp.exp2((scores - top) * RATE)
    total = jnp.sum(weights, axis=-1, keepdims=True)
    weights = weights.astype(jnp.bfloat16).reshape(g * TOK, -1)
    mixed = jnp.dot(weights, v, preferred_element_type=jnp.float32)
    return mixed.reshape(g, TOK, HD) / total


def student_head(pairs, first, sources, o_ref, o_at):
    (q_ref, q_at), (k_ref, k_at), (v_ref, v_at) = sources
    for i in pairs:
        width = (i + 2) * TOK
        block = lax.broadcasted_iota(jnp.int32, (2, 1, width), 2) // TOK
        own = lax.broadcasted_iota(jnp.int32, (2, 1, width), 0) + i
        bias = jnp.where((block == own) | (block >= first) & (block < own), 0.0, NEG)
        k = k_ref[0 : i + 2, k_at].reshape(width, HD)
        v = v_ref[0 : i + 2, v_at].reshape(width, HD)
        o_ref[i : i + 2, o_at] = attend(q_ref[i : i + 2, q_at], k, v, bias).astype(jnp.bfloat16)


def teacher_head(blocks, rows, clip_ref, sources, gen, o_ref, o_at):
    (q_ref, q_at), (k_ref, k_at) = sources
    reach = blocks // 2 + 1
    width = reach * TOK
    offset = lax.broadcasted_iota(jnp.int32, (1, 1, width), 2) // TOK
    for i in rows:
        low = clip_ref[0, i]
        high = clip_ref[1, i]
        start = jnp.minimum(low, blocks - reach)
        block = offset + start
        bias = jnp.where((block >= low) & (block < high), 0.0, NEG)
        k = k_ref[pl.ds(start, reach), k_at].reshape(width, HD)
        v = gen(pl.ds(start, reach)).reshape(width, HD)
        out = attend(q_ref[pl.ds(i, 1), q_at], k, v, bias)
        score = (out[0] - gen(i).astype(jnp.float32)).astype(jnp.bfloat16)
        if o_at is None:
            o_ref[1] = score
        else:
            o_ref[i, o_at] = score


def teacher_whole_head(blocks, clip_ref, sources, gen, o_ref, o_at):
    (q_ref, q_at), (k_ref, k_at) = sources
    reach = blocks // 2 + 1

    def put(at, out):
        score = out - gen(at).astype(jnp.float32)
        o_ref[at, o_at] = score.astype(jnp.bfloat16)

    large = clip_ref[2, 0]
    k = k_ref[pl.ds(large, reach), k_at].reshape(reach * TOK, HD)
    v = gen(pl.ds(large, reach)).reshape(reach * TOK, HD)
    for i in range(0, reach, 2):
        at = pl.ds(large + i, min(2, reach - i))
        put(at, attend(q_ref[at, q_at], k, v, None))
    span = blocks - reach - 1
    offset = lax.broadcasted_iota(jnp.int32, (1, 1, span * TOK), 2) // TOK
    for j in range(blocks - reach):
        i = jnp.where(j < large, j, j + reach)
        low, high = clip_ref[0, i], clip_ref[1, i]
        start = jnp.minimum(low, blocks - span)
        block = offset + start
        bias = jnp.where((block >= low) & (block < high), 0.0, NEG)
        k = k_ref[pl.ds(start, span), k_at].reshape(span * TOK, HD)
        v = gen(pl.ds(start, span)).reshape(span * TOK, HD)
        put(pl.ds(i, 1), attend(q_ref[pl.ds(i, 1), q_at], k, v, bias))


def cost(heads, blocks, units):
    return pl.CostEstimate(
        flops=heads * blocks * blocks * 4 * TOK * TOK * HD,
        bytes_accessed=units * blocks * TOK * HD * 2,
        transcendentals=heads * blocks * blocks * TOK * TOK,
    )


def pack(plan, ranges, tensors):
    peers, units = len(plan), len(plan[0])
    widths = [count * HD for _, count in ranges]
    starts = [sum(widths[:r]) for r in range(len(ranges))]

    def place(h):
        for r, (head, count) in enumerate(ranges):
            if head <= h < head + count:
                return r, starts[r] + (h - head) * HD

    need = []
    for u in range(units):
        need.append(list(dict.fromkeys((plan[p][u][0], place(plan[p][u][1])[0]) for p in range(peers))))
    order = sorted(range(units), key=lambda u: (len(need[u]), u))
    fetch = list(dict.fromkeys(piece for u in order for piece in need[u]))

    def body(*refs):
        o_ref, rows, tiles, in_sem, out_sem = refs[len(tensors) :]
        copies = {}
        for n, (t, r) in enumerate(fetch):
            source = refs[t].at[0, :, pl.ds(ranges[r][0] * HD, widths[r])]
            target = rows.at[t, :, pl.ds(starts[r], widths[r])]
            copies[t, r] = pltpu.make_async_copy(source, target, in_sem.at[n])
            copies[t, r].start()
        sent = []
        for u in order:
            for piece in need[u]:
                if piece in copies:
                    copies.pop(piece).wait()
            for p in range(peers):
                t, h = plan[p][u]
                at = place(h)[1]
                tiles[p, u] = rows[t, :, at : at + HD]
            sent.append(pltpu.make_async_copy(tiles.at[:, u], o_ref.at[:, u], out_sem.at[u]))
            sent[-1].start()
        for copy in sent:
            copy.wait()

    return pl.pallas_call(
        body,
        in_specs=[pl.BlockSpec(memory_space=pl.ANY)] * len(tensors),
        out_specs=pl.BlockSpec(memory_space=pl.ANY),
        out_shape=jax.ShapeDtypeStruct((peers, units, TOK, HD), jnp.bfloat16),
        scratch_shapes=[
            pltpu.VMEM((len(tensors), TOK, sum(widths)), jnp.bfloat16),
            pltpu.VMEM((peers, units, TOK, HD), jnp.bfloat16),
            pltpu.SemaphoreType.DMA((len(fetch),)),
            pltpu.SemaphoreType.DMA((units,)),
        ],
        compiler_params=WHOLE,
        cost_estimate=cost(0, peers, 2 * units),
    )(*tensors)


def unpack(places, back):
    def body(x_ref, *o_refs):
        for o_ref, place in zip(o_refs, places):
            for h, (p, u) in enumerate(place):
                o_ref[0, :, h * HD : (h + 1) * HD] = x_ref[p, u]

    width = len(places[0]) * HD
    return pl.pallas_call(
        body,
        out_shape=[jax.ShapeDtypeStruct((1, TOK, width), jnp.bfloat16) for _ in places],
        compiler_params=LOCAL,
        cost_estimate=cost(0, 1, 4 * len(places[0])),
    )(back)


def student_kernel(blocks, first, role, arrived):
    def body(first_ref, role_ref, x_ref, o_ref):
        @pl.when(role_ref[0] == 1)
        def _():
            sources = [(x_ref, t) for t in range(3)]
            student_head(range(0, blocks, 2), first_ref[0], sources, o_ref, 0)

    return pl.pallas_call(
        body,
        in_specs=[SMEM, SMEM, VMEM],
        out_specs=VMEM,
        out_shape=jax.ShapeDtypeStruct((blocks, 1, TOK, HD), jnp.bfloat16),
        compiler_params=LOCAL,
        cost_estimate=cost(1, blocks, 4),
    )(first, role, arrived)


def rest_teacher(blocks, clips, role, arrived, offset, gen, shared):
    def body(clip_ref, role_ref, x_ref, gen_ref, shared_ref, o_ref):
        @pl.when(role_ref[0] == 1)
        def _():
            o_ref[...] = gen_ref[...]

        @pl.when(role_ref[0] == 2)
        def _():
            sources = [(x_ref, offset + t) for t in range(2)]
            teacher_head(
                blocks, range(blocks), clip_ref, sources, lambda at: shared_ref[at, 0], o_ref, 0
            )

    return pl.pallas_call(
        body,
        in_specs=[SMEM, SMEM, VMEM, VMEM, VMEM],
        out_specs=VMEM,
        out_shape=jax.ShapeDtypeStruct((blocks, 1, TOK, HD), jnp.bfloat16),
        compiler_params=LOCAL,
        cost_estimate=cost(1, blocks, 5),
    )(clips, role, arrived, gen, shared)


def slots_kernel(full, blocks, first, clips, arrived):
    def body(first_ref, clip_ref, x_ref, o_ref):
        def head(s, carry):
            sources = [(x_ref, 5 * s + t) for t in range(5)]
            student_head(range(0, blocks, 2), first_ref[0], sources[:3], o_ref, 2 * s)
            gen = lambda at: o_ref[at, 2 * s]
            teacher_whole_head(blocks, clip_ref, sources[3:], gen, o_ref, 2 * s + 1)

        lax.fori_loop(0, full, head, None)

    return pl.pallas_call(
        body,
        in_specs=[SMEM, SMEM, VMEM],
        out_specs=VMEM,
        out_shape=jax.ShapeDtypeStruct((blocks, 2 * full, TOK, HD), jnp.bfloat16),
        compiler_params=LOCAL,
        cost_estimate=cost(2 * full, blocks, 7 * full),
    )(first, clips, arrived)


def rest_pack(base, columns, column, tensors):
    def body(column_ref, *refs):
        rows, sems = refs[-2:]
        copies = []
        for t in range(5):
            source = refs[t].at[0, :, pl.ds(base * HD, columns * HD)]
            copies.append(pltpu.make_async_copy(source, rows.at[t], sems.at[t]))
            copies[-1].start()
        for t in range(5):
            copies[t].wait()
            for s in range(columns):
                at = pl.multiple_of((column_ref[0] ^ s) * HD, HD)
                refs[5 + s][t] = rows[t, :, pl.ds(at, HD)]

    return pl.pallas_call(
        body,
        in_specs=[SMEM] + [pl.BlockSpec(memory_space=pl.ANY)] * 5,
        out_specs=[VMEM] * columns,
        out_shape=[jax.ShapeDtypeStruct((5, TOK, HD), jnp.bfloat16)] * columns,
        scratch_shapes=[
            pltpu.VMEM((5, TOK, columns * HD), jnp.bfloat16),
            pltpu.SemaphoreType.DMA((5,)),
        ],
        compiler_params=WHOLE,
        cost_estimate=cost(0, 1, 10 * columns),
    )(column, *tensors)


def rest_kernel(columns, first, clips, where, own, other):
    blocks = 2 * columns

    def body(first_ref, clip_ref, where_ref, *refs):
        x, gen = refs[-2:]
        column, side = where_ref[0], where_ref[1]
        mine = [2 * (column ^ s) + side for s in range(columns)]
        for s in range(columns):
            x[mine[s]] = refs[s][...]
            x[mine[s] ^ 1] = refs[columns + s][...]
        sources = [(x, t) for t in range(5)]
        student_head(range(0, blocks, 2), first_ref[0], sources[:3], gen, 0)
        at_gen = lambda at: gen[at, 0]
        for s in range(columns):
            o_ref = refs[2 * columns + s]
            o_ref[0:1] = gen[mine[s]]
            teacher_head(blocks, [mine[s]], clip_ref, sources[3:], at_gen, o_ref, None)

    return pl.pallas_call(
        body,
        in_specs=[SMEM] * 3 + [VMEM] * (2 * columns),
        out_specs=[VMEM] * columns,
        out_shape=[jax.ShapeDtypeStruct((2, TOK, HD), jnp.bfloat16)] * columns,
        scratch_shapes=[
            pltpu.VMEM((blocks, 5, TOK, HD), jnp.bfloat16),
            pltpu.VMEM((blocks, 1, TOK, HD), jnp.bfloat16),
        ],
        compiler_params=LOCAL,
        cost_estimate=cost(2, blocks, 7),
    )(first, clips, where, *own, *other)


def join(base, columns, places, column, back, pieces):
    def body(column_ref, x_ref, *refs):
        for i, o_ref in enumerate(refs[columns:]):
            for h, (p, u) in enumerate(places[i]):
                o_ref[0, :, h * HD : (h + 1) * HD] = x_ref[p, u]
            for s in range(columns):
                at = pl.multiple_of((base + (column_ref[0] ^ s)) * HD, HD)
                o_ref[0, :, pl.ds(at, HD)] = refs[s][i]

    width = (base + columns) * HD
    return pl.pallas_call(
        body,
        in_specs=[SMEM, VMEM] + [VMEM] * columns,
        out_specs=[VMEM] * 2,
        out_shape=[jax.ShapeDtypeStruct((1, TOK, width), jnp.bfloat16)] * 2,
        compiler_params=LOCAL,
        cost_estimate=cost(0, 1, 4 * (base + columns)),
    )(column, back, *pieces)


def by_slots_and_columns(tensors, peers, full, rest, first, clips):
    base = full * peers
    here = lax.axis_index("tm")
    column, side = here // 2, here % 2
    where = jnp.stack([column, side]).astype(jnp.int32)

    def swapped(x, by):
        return lax.ppermute(x, "tm", [(i, i ^ by) for i in range(peers)])

    plan = [[(t, s * peers + p) for s in range(full) for t in range(5)] for p in range(peers)]
    slots = [(s * peers, peers) for s in range(full)]
    pieces = rest_pack(base, rest, where[:1], tensors)
    own = [swapped(x, 2 * s) if s else x for s, x in enumerate(pieces)]
    other = [swapped(x, 1) for x in own]
    packed, _ = lax.optimization_barrier((pack(plan, slots, tensors), own))
    arrived = lax.all_to_all(packed, "tm", 0, 0)
    pieces = rest_kernel(rest, first, clips, where, own, other)
    arrived, _ = lax.optimization_barrier((arrived, pieces))
    results = slots_kernel(full, peers, first, clips, arrived)
    pieces = [swapped(x, 2 * s) if s else x for s, x in enumerate(pieces)]
    results, pieces = lax.optimization_barrier((results, pieces))
    back = lax.all_to_all(results, "tm", 0, 0)
    places = [[(h % peers, 2 * (h // peers) + i) for h in range(base)] for i in (0, 1)]
    return tuple(join(base, rest, places, where[:1], back, pieces))


def by_roles(tensors, peers, heads, first, clips):
    here = lax.axis_index("tm")
    role = jnp.where(here < 2 * heads, 1 + here % 2, 0).astype(jnp.int32)[None]
    plan = [
        [(t, min(p // 2, heads - 1)) for t in ((3, 4, 4) if p % 2 else (0, 1, 2))]
        for p in range(peers)
    ]
    arrived = lax.all_to_all(pack(plan, [(0, heads)], tensors), "tm", 0, 0)
    gen = student_kernel(peers, first, role, arrived)
    shared = lax.ppermute(gen, "tm", [(2 * r, 2 * r + 1) for r in range(heads)])
    results = rest_teacher(peers, clips, role, arrived, 0, gen, shared)
    back = lax.all_to_all(results, "tm", 0, 0)
    return tuple(unpack([[(2 * r + i, 0) for r in range(heads)] for i in (0, 1)], back))


def per_device(student_q, student_k, student_v, teacher_q, teacher_k, stagger, clip_lengths):
    heads = student_q.shape[2] // HD
    peers = lax.axis_size("tm")
    full, rest = divmod(heads, peers)
    running = jnp.cumsum(clip_lengths[0])
    block = jnp.arange(peers, dtype=jnp.int32)
    before = running[None, :] <= block[:, None]
    low = jnp.max(jnp.where(before, running[None, :], 0), axis=1)
    high = jnp.min(jnp.where(before, peers, running[None, :]), axis=1)
    large = jnp.where(clip_lengths[0] == peers // 2 + 1, running - clip_lengths[0], 0)
    large = jnp.broadcast_to(jnp.max(large), (peers,))
    clips = jnp.stack([low, high, large]).astype(jnp.int32)
    tensors = (student_q, student_k, student_v, teacher_q, teacher_k)
    if full == 0:
        assert 2 * rest <= peers
        return by_roles(tensors, peers, rest, stagger, clips)
    assert peers == 2 * rest and rest & (rest - 1) == 0
    return by_slots_and_columns(tensors, peers, full, rest, stagger, clips)


def solution(mesh):
    spec = P("seq", "tm", "mp")
    return jax.shard_map(
        per_device,
        mesh=mesh,
        in_specs=(spec,) * 5 + (P("seq"), P("seq", None)),
        out_specs=(spec, spec),
        check_vma=False,
    )
```

profile of v0, /device:TPU:0, one launch (start us, length us, event | category | flops | bytes accessed | tf_op | source)
XLA Modules:
  0.0 126.5 jit_solution(6957079355361200920)
XLA Ops:
  0.6 2.1 %shard_map.87 = (bf16[5,128,128]{2,1,0:T(8,128)(2,1)}, bf16[5,128,128]{2,1,0:T(8,128)(2,1)}, bf16[5,128,128]{2,1,0:T(8,128)(2,1)}, bf16[5,128,128]{2,1,0:T(8,128)(2,1)}) custom-call(s32[1]{0:T(128)} %bitcast.column_ref, bf16[1,128,2560]{2,1,0:T(8,128)(2,1)} %refs_0_.3, bf16[1,128,2560]{2,1,0:T(8,128)(2,1)} %refs_1_.3, bf16[1,128,2560]{2,1,0:T(8,128)(2,1)} %refs_2_.3, ...), custom_call_target="tpu_custom_call" | custom-call | bytes 1310720 | tf_op jit(solution)/shard_map/pallas_call | solution.py:249
  2.7 3.1 %collective-permute-start = (bf16[5,128,128]{2,1,0:T(8,128)(2,1)}, bf16[5,128,128]{2,1,0:T(8,128)(2,1)S(1)}, u32[]{:S(2)}, u32[]{:S(2)}) collective-permute-start(bf16[5,128,128]{2,1,0:T(8,128)(2,1)} %get-tuple-element.18), channel_id=1, source_target_pairs={{0,8},{4,12},{8,0},{12,4},{16,24},{20,28},{24,16},{28,20},{1,9},{5... | collective-permute-start | bytes 491528 | tf_op jit(solution)/shard_map/ppermute | solution.py:322
  5.8 2.6 %collective-permute-start.1 = (bf16[5,128,128]{2,1,0:T(8,128)(2,1)}, bf16[5,128,128]{2,1,0:T(8,128)(2,1)S(1)}, u32[]{:S(2)}, u32[]{:S(2)}) collective-permute-start(bf16[5,128,128]{2,1,0:T(8,128)(2,1)} %get-tuple-element.19), channel_id=1, source_target_pairs={{0,16},{4,20},{8,24},{12,28},{16,0},{20,4},{24,8},{28,12},{1,17},{... | collective-permute-start | bytes 491528 | tf_op jit(solution)/shard_map/ppermute | solution.py:322
  8.4 0.0 collective-permute-start.2
  8.4 2.7 %shard_map.86 = bf16[8,10,128,128]{3,2,1,0:T(8,128)(2,1)} custom-call(bf16[1,128,2560]{2,1,0:T(8,128)(2,1)} %refs_0_.3, bf16[1,128,2560]{2,1,0:T(8,128)(2,1)} %refs_1_.3, bf16[1,128,2560]{2,1,0:T(8,128)(2,1)} %refs_2_.3, bf16[1,128,2560]{2,1,0:T(8,128)(2,1)} %refs_3_.3, bf16[1,128,2560]{2,1,0:T(8,128)(2,1)} %refs_4_.3), custom_call_target="tpu_custom_call" | custom-call | bytes 5242880 | tf_op jit(solution)/shard_map/pallas_call | solution.py:144
  11.1 1.6 %collective-permute-done.refs_1_ = bf16[5,128,128]{2,1,0:T(8,128)(2,1)S(1)} collective-permute-done((bf16[5,128,128]{2,1,0:T(8,128)(2,1)}, bf16[5,128,128]{2,1,0:T(8,128)(2,1)S(1)}, u32[]{:S(2)}, u32[]{:S(2)}) %collective-permute-start) | collective-permute-done | bytes 163872 | tf_op jit(solution)/shard_map/ppermute | solution.py:322
  12.7 8.4 %collective-permute-done.1.refs_2_ = bf16[5,128,128]{2,1,0:T(8,128)(2,1)S(1)} collective-permute-done((bf16[5,128,128]{2,1,0:T(8,128)(2,1)}, bf16[5,128,128]{2,1,0:T(8,128)(2,1)S(1)}, u32[]{:S(2)}, u32[]{:S(2)}) %collective-permute-start.1) | collective-permute-done | bytes 163872 | tf_op jit(solution)/shard_map/ppermute | solution.py:322
  21.1 0.0 collective-permute-done.2.refs_3_
  21.1 0.0 copy-start
  21.1 0.0 copy-start.1
  21.1 6.0 %all-to-all-start = ((bf16[8,10,128,128]{3,2,1,0:T(8,128)(2,1)}), bf16[8,10,128,128]{3,2,1,0:T(8,128)(2,1)S(1)}, u32[]{:S(2)}, u32[]{:S(2)}) async-start(bf16[8,10,128,128]{3,2,1,0:T(8,128)(2,1)} %shard_map.86), calls=%async_computation | async-start | bytes 5242880 | tf_op jit(solution)/shard_map/all_to_all | solution.py:330
  27.1 0.0 copy-done
  27.1 2.0 %collective-permute-start.3 = (bf16[5,128,128]{2,1,0:T(8,128)(2,1)S(1)}, bf16[5,128,128]{2,1,0:T(8,128)(2,1)S(1)}, u32[]{:S(2)}, u32[]{:S(2)}) collective-permute-start(bf16[5,128,128]{2,1,0:T(8,128)(2,1)S(1)} %copy-done), channel_id=1, source_target_pairs={{0,4},{4,0},{8,12},{12,8},{16,20},{20,16},{24,28},{28,24},{1,5},{5... | collective-permute-start | bytes 491528 | tf_op jit(solution)/shard_map/ppermute | solution.py:322
  29.1 0.0 copy-done.1
  29.1 0.2 reduce-window.8
  29.3 0.6 fusion
  29.9 0.7 pad.4.clone
  30.6 0.1 select_reduce_fusion.1
  30.7 0.1 collective-permute-start.4
  30.8 2.0 %collective-permute-start.5 = (bf16[5,128,128]{2,1,0:T(8,128)(2,1)S(1)}, bf16[5,128,128]{2,1,0:T(8,128)(2,1)}, u32[]{:S(2)}, u32[]{:S(2)}) collective-permute-start(bf16[5,128,128]{2,1,0:T(8,128)(2,1)S(1)} %collective-permute-done.1.refs_2_), channel_id=1, source_target_pairs={{0,4},{4,0},{8,12},{12,8},{16,20},{20,16},{24,28},{28,24},{1,5},{5... | collective-permute-start | bytes 491528 | tf_op jit(solution)/shard_map/ppermute | solution.py:322
  32.8 0.1 collective-permute-start.6
  32.9 0.1 add_add_fusion.clip_ref
  33.6 0.1 pad_add_fusion.where_ref
  33.7 20.2 %collective-permute-done.3.refs_4_ = bf16[5,128,128]{2,1,0:T(8,128)(2,1)S(1)} collective-permute-done((bf16[5,128,128]{2,1,0:T(8,128)(2,1)S(1)}, bf16[5,128,128]{2,1,0:T(8,128)(2,1)S(1)}, u32[]{:S(2)}, u32[]{:S(2)}) %collective-permute-start.3) | collective-permute-done | bytes 163872 | tf_op jit(solution)/shard_map/ppermute | solution.py:322
  53.9 6.3 %collective-permute-done.4.refs_5_ = bf16[5,128,128]{2,1,0:T(8,128)(2,1)} collective-permute-done((bf16[5,128,128]{2,1,0:T(8,128)(2,1)S(1)}, bf16[5,128,128]{2,1,0:T(8,128)(2,1)}, u32[]{:S(2)}, u32[]{:S(2)}) %collective-permute-start.4) | collective-permute-done | bytes 163872 | tf_op jit(solution)/shard_map/ppermute | solution.py:322
  60.2 8.6 %collective-permute-done.5.refs_6_ = bf16[5,128,128]{2,1,0:T(8,128)(2,1)} collective-permute-done((bf16[5,128,128]{2,1,0:T(8,128)(2,1)S(1)}, bf16[5,128,128]{2,1,0:T(8,128)(2,1)}, u32[]{:S(2)}, u32[]{:S(2)}) %collective-permute-start.5) | collective-permute-done | bytes 163872 | tf_op jit(solution)/shard_map/ppermute | solution.py:322
  68.8 1.8 %collective-permute-done.6.refs_7_ = bf16[5,128,128]{2,1,0:T(8,128)(2,1)} collective-permute-done((bf16[5,128,128]{2,1,0:T(8,128)(2,1)S(1)}, bf16[5,128,128]{2,1,0:T(8,128)(2,1)}, u32[]{:S(2)}, u32[]{:S(2)}) %collective-permute-start.6) | collective-permute-done | bytes 163872 | tf_op jit(solution)/shard_map/ppermute | solution.py:322
  70.7 4.7 %shard_map.88 = (bf16[2,128,128]{2,1,0:T(8,128)(2,1)S(1)}, bf16[2,128,128]{2,1,0:T(8,128)(2,1)}, bf16[2,128,128]{2,1,0:T(8,128)(2,1)}, bf16[2,128,128]{2,1,0:T(8,128)(2,1)}) custom-call(s32[1]{0:T(128)S(6)} %copy.9.first_ref, s32[3,8]{1,0:T(4,128)S(1)} %add_add_fusion.clip_ref, s32[2]{0:T(128)S(1)} %pad_add_fusion.where_ref, ...), custom_call_target="tpu_custom_call" | custom-call | flops 1073741824 | bytes 1835008 | tf_op jit(solution)/shard_map/pallas_call | solution.py:281
  75.4 0.0 collective-permute-start.7
  75.4 3.8 %collective-permute-start.8 = (bf16[2,128,128]{2,1,0:T(8,128)(2,1)}, bf16[2,128,128]{2,1,0:T(8,128)(2,1)S(1)}, u32[]{:S(2)}, u32[]{:S(2)}) collective-permute-start(bf16[2,128,128]{2,1,0:T(8,128)(2,1)} %get-tuple-element.24), channel_id=1, source_target_pairs={{0,16},{4,20},{8,24},{12,28},{16,0},{20,4},{24,8},{28,12},{1,17},{... | collective-permute-start | bytes 196616 | tf_op jit(solution)/shard_map/ppermute | solution.py:322
  79.2 0.6 collective-permute-start.9
  79.8 10.1 %all-to-all-done.x_ref = bf16[8,10,128,128]{3,2,1,0:T(8,128)(2,1)S(1)} async-done(((bf16[8,10,128,128]{3,2,1,0:T(8,128)(2,1)}), bf16[8,10,128,128]{3,2,1,0:T(8,128)(2,1)S(1)}, u32[]{:S(2)}, u32[]{:S(2)}) %all-to-all-start) | async-done | bytes 2621472 | tf_op jit(solution)/shard_map/all_to_all | solution.py:330
  89.9 7.3 %shard_map.89 = bf16[8,4,128,128]{3,2,1,0:T(8,128)(2,1)S(1)} custom-call(s32[1]{0:T(128)S(6)} %copy.9.first_ref, s32[3,8]{1,0:T(4,128)S(1)} %add_add_fusion.clip_ref, bf16[8,10,128,128]{3,2,1,0:T(8,128)(2,1)S(1)} %all-to-all-done.x_ref), custom_call_target="tpu_custom_call" | custom-call | flops 2147483648 | bytes 3670016 | tf_op jit(solution)/shard_map/pallas_call | solution.py:225
  97.2 0.0 collective-permute-done.7.refs_1_
  97.2 0.0 collective-permute-done.8.refs_2_
  97.2 0.0 collective-permute-done.9.refs_3_
  97.2 28.0 %all_to_all.10.x_ref = bf16[8,4,128,128]{3,2,1,0:T(8,128)(2,1)S(1)} all-to-all(bf16[8,4,128,128]{3,2,1,0:T(8,128)(2,1)S(1)} %shard_map.89), channel_id=1, replica_groups=mesh['tm'=8,'seq'=2,'mp'=2] {'tm'}, dimensions={0} | all-to-all | bytes 2097152 | tf_op jit(solution)/shard_map/all_to_all | solution.py:336
  125.2 1.3 %shard_map.90 = (bf16[1,128,2560]{2,1,0:T(8,128)(2,1)}, bf16[1,128,2560]{2,1,0:T(8,128)(2,1)}) custom-call(s32[1]{0:T(128)} %bitcast.column_ref, bf16[8,4,128,128]{3,2,1,0:T(8,128)(2,1)S(1)} %all_to_all.10.x_ref, bf16[2,128,128]{2,1,0:T(8,128)(2,1)S(1)} %get-tuple-element.28.refs_0_, bf16[2,128,128]{2,1,0:T(8,128)(2,1)S(1)} %collective-permute-done.7.refs_1_, ...), custom_call_target="tpu_custom_call" | custom-call | bytes 2621440 | tf_op jit(solution)/shard_map/pallas_call | solution.py:305
Async XLA Ops:
  2.7 10.0 %collective-permute-start = (bf16[5,128,128]{2,1,0:T(8,128)(2,1)}, bf16[5,128,128]{2,1,0:T(8,128)(2,1)S(1)}, u32[]{:S(2)}, u32[]{:S(2)}) collective-permute-start(bf16[5,128,128]{2,1,0:T(8,128)(2,1)} %get-tuple-element.18), channel_id=1, source_target_pairs={{0,8},{4,12},{8,0},{12,4},{16,24},{20,28},{24,16},{28,20},{1,9},{5... | collective-permute-start | bytes 491528 | tf_op jit(solution)/shard_map/ppermute | solution.py:322
  5.8 15.3 %collective-permute-start.1 = (bf16[5,128,128]{2,1,0:T(8,128)(2,1)}, bf16[5,128,128]{2,1,0:T(8,128)(2,1)S(1)}, u32[]{:S(2)}, u32[]{:S(2)}) collective-permute-start(bf16[5,128,128]{2,1,0:T(8,128)(2,1)} %get-tuple-element.19), channel_id=1, source_target_pairs={{0,16},{4,20},{8,24},{12,28},{16,0},{20,4},{24,8},{28,12},{1,17},{... | collective-permute-start | bytes 491528 | tf_op jit(solution)/shard_map/ppermute | solution.py:322
  8.4 12.7 %collective-permute-start.2 = (bf16[5,128,128]{2,1,0:T(8,128)(2,1)}, bf16[5,128,128]{2,1,0:T(8,128)(2,1)S(1)}, u32[]{:S(2)}, u32[]{:S(2)}) collective-permute-start(bf16[5,128,128]{2,1,0:T(8,128)(2,1)} %get-tuple-element.20), channel_id=1, source_target_pairs={{0,24},{4,28},{8,16},{12,20},{16,8},{20,12},{24,0},{28,4},{1,25},{... | collective-permute-start | bytes 491528 | tf_op jit(solution)/shard_map/ppermute | solution.py:322
  21.1 6.0 %copy-start = (bf16[5,128,128]{2,1,0:T(8,128)(2,1)S(1)}, bf16[5,128,128]{2,1,0:T(8,128)(2,1)}, u32[]{:S(2)}) copy-start(bf16[5,128,128]{2,1,0:T(8,128)(2,1)} %get-tuple-element.17.refs_0_) | copy-start | bytes 491524
  21.1 8.0 %copy-start.1 = (s32[1,3]{1,0:T(1,128)S(1)}, s32[1,3]{1,0:T(1,128)}, u32[]{:S(2)}) copy-start(s32[1,3]{1,0:T(1,128)} %param.13) | copy-start | bytes 40
  21.1 68.8 %all-to-all-start = ((bf16[8,10,128,128]{3,2,1,0:T(8,128)(2,1)}), bf16[8,10,128,128]{3,2,1,0:T(8,128)(2,1)S(1)}, u32[]{:S(2)}, u32[]{:S(2)}) async-start(bf16[8,10,128,128]{3,2,1,0:T(8,128)(2,1)} %shard_map.86), calls=%async_computation | async-start | bytes 5242880 | tf_op jit(solution)/shard_map/all_to_all | solution.py:330
  27.1 26.8 %collective-permute-start.3 = (bf16[5,128,128]{2,1,0:T(8,128)(2,1)S(1)}, bf16[5,128,128]{2,1,0:T(8,128)(2,1)S(1)}, u32[]{:S(2)}, u32[]{:S(2)}) collective-permute-start(bf16[5,128,128]{2,1,0:T(8,128)(2,1)S(1)} %copy-done), channel_id=1, source_target_pairs={{0,4},{4,0},{8,12},{12,8},{16,20},{20,16},{24,28},{28,24},{1,5},{5... | collective-permute-start | bytes 491528 | tf_op jit(solution)/shard_map/ppermute | solution.py:322
  30.7 29.5 %collective-permute-start.4 = (bf16[5,128,128]{2,1,0:T(8,128)(2,1)S(1)}, bf16[5,128,128]{2,1,0:T(8,128)(2,1)}, u32[]{:S(2)}, u32[]{:S(2)}) collective-permute-start(bf16[5,128,128]{2,1,0:T(8,128)(2,1)S(1)} %collective-permute-done.refs_1_), channel_id=1, source_target_pairs={{0,4},{4,0},{8,12},{12,8},{16,20},{20,16},{24,28},{28,24},{1,5},{5... | collective-permute-start | bytes 491528 | tf_op jit(solution)/shard_map/ppermute | solution.py:322
  30.8 38.0 %collective-permute-start.5 = (bf16[5,128,128]{2,1,0:T(8,128)(2,1)S(1)}, bf16[5,128,128]{2,1,0:T(8,128)(2,1)}, u32[]{:S(2)}, u32[]{:S(2)}) collective-permute-start(bf16[5,128,128]{2,1,0:T(8,128)(2,1)S(1)} %collective-permute-done.1.refs_2_), channel_id=1, source_target_pairs={{0,4},{4,0},{8,12},{12,8},{16,20},{20,16},{24,28},{28,24},{1,5},{5... | collective-permute-start | bytes 491528 | tf_op jit(solution)/shard_map/ppermute | solution.py:322
  32.8 37.9 %collective-permute-start.6 = (bf16[5,128,128]{2,1,0:T(8,128)(2,1)S(1)}, bf16[5,128,128]{2,1,0:T(8,128)(2,1)}, u32[]{:S(2)}, u32[]{:S(2)}) collective-permute-start(bf16[5,128,128]{2,1,0:T(8,128)(2,1)S(1)} %collective-permute-done.2.refs_3_), channel_id=1, source_target_pairs={{0,4},{4,0},{8,12},{12,8},{16,20},{20,16},{24,28},{28,24},{1,5},{5... | collective-permute-start | bytes 491528 | tf_op jit(solution)/shard_map/ppermute | solution.py:322
  75.4 21.8 %collective-permute-start.7 = (bf16[2,128,128]{2,1,0:T(8,128)(2,1)}, bf16[2,128,128]{2,1,0:T(8,128)(2,1)S(1)}, u32[]{:S(2)}, u32[]{:S(2)}) collective-permute-start(bf16[2,128,128]{2,1,0:T(8,128)(2,1)} %get-tuple-element.23), channel_id=1, source_target_pairs={{0,8},{4,12},{8,0},{12,4},{16,24},{20,28},{24,16},{28,20},{1,9},{5... | collective-permute-start | bytes 196616 | tf_op jit(solution)/shard_map/ppermute | solution.py:322
  75.4 21.8 %collective-permute-start.8 = (bf16[2,128,128]{2,1,0:T(8,128)(2,1)}, bf16[2,128,128]{2,1,0:T(8,128)(2,1)S(1)}, u32[]{:S(2)}, u32[]{:S(2)}) collective-permute-start(bf16[2,128,128]{2,1,0:T(8,128)(2,1)} %get-tuple-element.24), channel_id=1, source_target_pairs={{0,16},{4,20},{8,24},{12,28},{16,0},{20,4},{24,8},{28,12},{1,17},{... | collective-permute-start | bytes 196616 | tf_op jit(solution)/shard_map/ppermute | solution.py:322
  79.2 18.0 %collective-permute-start.9 = (bf16[2,128,128]{2,1,0:T(8,128)(2,1)}, bf16[2,128,128]{2,1,0:T(8,128)(2,1)S(1)}, u32[]{:S(2)}, u32[]{:S(2)}) collective-permute-start(bf16[2,128,128]{2,1,0:T(8,128)(2,1)} %get-tuple-element.25), channel_id=1, source_target_pairs={{0,24},{4,28},{8,16},{12,20},{16,8},{20,12},{24,0},{28,4},{1,25},{... | collective-permute-start | bytes 196616 | tf_op jit(solution)/shard_map/ppermute | solution.py:322
where the time goes:
time: 127 us; the launch traced here: 126 us
  waiting for transfers between devices  57.1 us (45%)
  blocking collectives  28 us (22%)
  starting transfers between devices  20.2 us (16%)
  Pallas kernels  18 us (14%)
  between operations  1.36 us (1%)
    ppermute x10, waiting for transfers between devices, swapped(): return lax.ppermute(x, 'tm', [(i, i ^ by) for i in range(peers)])  47 us
    all_to_all x1, blocking collectives, by_slots_and_columns(): back = lax.all_to_all(results, 'tm', 0, 0)  28 us
    ppermute x10, starting transfers between devices, swapped(): return lax.ppermute(x, 'tm', [(i, i ^ by) for i in range(peers)])  14.3 us
    all_to_all x1, waiting for transfers between devices, by_slots_and_columns(): arrived = lax.all_to_all(packed, 'tm', 0, 0)  10.1 us
    pallas_call x1, Pallas kernels, slots_kernel(): pl.pallas_call(body, in_specs=[SMEM, SMEM, VMEM], out_specs=VMEM, out_sha...  7.28 us
    all_to_all x1, starting transfers between devices, by_slots_and_columns(): arrived = lax.all_to_all(packed, 'tm', 0, 0)  5.99 us
    pallas_call x1, Pallas kernels, rest_kernel(): pl.pallas_call(body, in_specs=[SMEM] * 3 + [VMEM] * (2 * columns), out_sp...  4.71 us
    pallas_call x1, Pallas kernels, pack(): pl.pallas_call(body, in_specs=[pl.BlockSpec(memory_space=pl.ANY)] * len(t...  2.66 us
  transfers between devices with their start and end apart: 11, of which 7 were waited for; matrix products, arithmetic and copies ran while one was open for 1% of the time, Pallas kernels for 12%

commit v1 on v0

--- a/solution.py
+++ b/solution.py
@@ -212,24 +212,64 @@
     )(clips, role, arrived, gen, shared)
 
 
-def slots_kernel(full, blocks, first, clips, arrived):
-    def body(first_ref, clip_ref, x_ref, o_ref):
+def slots_kernel(full, blocks, first, clips, where, arrived):
+    def body(first_ref, clip_ref, where_ref, *refs):
+        x_refs, o_refs, (x, y) = refs[:blocks], refs[blocks : 2 * blocks], refs[2 * blocks :]
+        at = [where_ref[2] ^ d for d in range(blocks)]
+        for d in range(blocks):
+            x[at[d]] = x_refs[d][...]
+
         def head(s, carry):
-            sources = [(x_ref, 5 * s + t) for t in range(5)]
-            student_head(range(0, blocks, 2), first_ref[0], sources[:3], o_ref, 2 * s)
-            gen = lambda at: o_ref[at, 2 * s]
-            teacher_whole_head(blocks, clip_ref, sources[3:], gen, o_ref, 2 * s + 1)
+            sources = [(x, 5 * s + t) for t in range(5)]
+            student_head(range(0, blocks, 2), first_ref[0], sources[:3], y, 2 * s)
+            gen = lambda at: y[at, 2 * s]
+            teacher_whole_head(blocks, clip_ref, sources[3:], gen, y, 2 * s + 1)
 
         lax.fori_loop(0, full, head, None)
-
-    return pl.pallas_call(
-        body,
-        in_specs=[SMEM, SMEM, VMEM],
-        out_specs=VMEM,
-        out_shape=jax.ShapeDtypeStruct((blocks, 2 * full, TOK, HD), jnp.bfloat16),
+        for d in range(blocks):
+            o_refs[d][...] = y[at[d]]
+
+    return pl.pallas_call(
+        body,
+        in_specs=[SMEM] * 3 + [VMEM] * blocks,
+        out_specs=[VMEM] * blocks,
+        out_shape=[jax.ShapeDtypeStruct((2 * full, TOK, HD), jnp.bfloat16)] * blocks,
+        scratch_shapes=[
+            pltpu.VMEM((blocks, 5 * full, TOK, HD), jnp.bfloat16),
+            pltpu.VMEM((blocks, 2 * full, TOK, HD), jnp.bfloat16),
+        ],
         compiler_params=LOCAL,
         cost_estimate=cost(2 * full, blocks, 7 * full),
-    )(first, clips, arrived)
+    )(first, clips, where, *arrived)
+
+
+def slots_pack(full, peers, where, tensors):
+    def body(where_ref, *refs):
+        o_refs, (rows, sems) = refs[5 : 5 + peers], refs[5 + peers :]
+        copies = []
+        for t in range(5):
+            source = refs[t].at[0, :, pl.ds(0, full * peers * HD)]
+            copies.append(pltpu.make_async_copy(source, rows.at[t], sems.at[t]))
+            copies[-1].start()
+        for t in range(5):
+            copies[t].wait()
+            for s in range(full):
+                for d in range(peers):
+                    at = pl.multiple_of((s * peers + (where_ref[2] ^ d)) * HD, HD)
+                    o_refs[d][5 * s + t] = rows[t, :, pl.ds(at, HD)]
+
+    return pl.pallas_call(
+        body,
+        in_specs=[SMEM] + [pl.BlockSpec(memory_space=pl.ANY)] * 5,
+        out_specs=[VMEM] * peers,
+        out_shape=[jax.ShapeDtypeStruct((5 * full, TOK, HD), jnp.bfloat16)] * peers,
+        scratch_shapes=[
+            pltpu.VMEM((5, TOK, full * peers * HD), jnp.bfloat16),
+            pltpu.SemaphoreType.DMA((5,)),
+        ],
+        compiler_params=WHOLE,
+        cost_estimate=cost(0, peers, 10 * full),
+    )(where, *tensors)
 
 
 def rest_pack(base, columns, column, tensors):
@@ -292,50 +332,50 @@
     )(first, clips, where, *own, *other)
 
 
-def join(base, columns, places, column, back, pieces):
-    def body(column_ref, x_ref, *refs):
-        for i, o_ref in enumerate(refs[columns:]):
-            for h, (p, u) in enumerate(places[i]):
-                o_ref[0, :, h * HD : (h + 1) * HD] = x_ref[p, u]
+def join(full, peers, columns, where, slots, rests):
+    def body(where_ref, *refs):
+        for i, o_ref in enumerate(refs[peers + columns :]):
+
+            def put(h, tile):
+                o_ref[0, :, pl.ds(pl.multiple_of(h * HD, HD), HD)] = tile
+
+            for d in range(peers):
+                for s in range(full):
+                    put(s * peers + (where_ref[2] ^ d), refs[d][2 * s + i])
             for s in range(columns):
-                at = pl.multiple_of((base + (column_ref[0] ^ s)) * HD, HD)
-                o_ref[0, :, pl.ds(at, HD)] = refs[s][i]
-
-    width = (base + columns) * HD
-    return pl.pallas_call(
-        body,
-        in_specs=[SMEM, VMEM] + [VMEM] * columns,
+                put(full * peers + (where_ref[0] ^ s), refs[peers + s][i])
+
+    width = (full * peers + columns) * HD
+    return pl.pallas_call(
+        body,
+        in_specs=[SMEM] + [VMEM] * (peers + columns),
         out_specs=[VMEM] * 2,
         out_shape=[jax.ShapeDtypeStruct((1, TOK, width), jnp.bfloat16)] * 2,
         compiler_params=LOCAL,
-        cost_estimate=cost(0, 1, 4 * (base + columns)),
-    )(column, back, *pieces)
+        cost_estimate=cost(0, 1, 4 * width // HD),
+    )(where, *slots, *rests)
 
 
 def by_slots_and_columns(tensors, peers, full, rest, first, clips):
-    base = full * peers
     here = lax.axis_index("tm")
-    column, side = here // 2, here % 2
-    where = jnp.stack([column, side]).astype(jnp.int32)
+    where = jnp.stack([here // 2, here % 2, here]).astype(jnp.int32)
 
     def swapped(x, by):
-        return lax.ppermute(x, "tm", [(i, i ^ by) for i in range(peers)])
-
-    plan = [[(t, s * peers + p) for s in range(full) for t in range(5)] for p in range(peers)]
-    slots = [(s * peers, peers) for s in range(full)]
-    pieces = rest_pack(base, rest, where[:1], tensors)
-    own = [swapped(x, 2 * s) if s else x for s, x in enumerate(pieces)]
+        return lax.ppermute(x, "tm", [(i, i ^ by) for i in range(peers)]) if by else x
+
+    pieces = rest_pack(full * peers, rest, where[:1], tensors)
+    own = [swapped(x, 2 * s) for s, x in enumerate(pieces)]
+    packed = slots_pack(full, peers, where, tensors)
+    packed, own = lax.optimization_barrier((packed, own))
+    arrived = [swapped(x, d) for d, x in enumerate(packed)]
     other = [swapped(x, 1) for x in own]
-    packed, _ = lax.optimization_barrier((pack(plan, slots, tensors), own))
-    arrived = lax.all_to_all(packed, "tm", 0, 0)
     pieces = rest_kernel(rest, first, clips, where, own, other)
-    arrived, _ = lax.optimization_barrier((arrived, pieces))
-    results = slots_kernel(full, peers, first, clips, arrived)
-    pieces = [swapped(x, 2 * s) if s else x for s, x in enumerate(pieces)]
-    results, pieces = lax.optimization_barrier((results, pieces))
-    back = lax.all_to_all(results, "tm", 0, 0)
-    places = [[(h % peers, 2 * (h // peers) + i) for h in range(base)] for i in (0, 1)]
-    return tuple(join(base, rest, places, where[:1], back, pieces))
+    arrived, pieces = lax.optimization_barrier((arrived, pieces))
+    rests = [swapped(x, 2 * s) for s, x in enumerate(pieces)]
+    results = slots_kernel(full, peers, first, clips, where, arrived)
+    results, rests = lax.optimization_barrier((results, rests))
+    slots = [swapped(x, d) for d, x in enumerate(results)]
+    return tuple(join(full, peers, rest, where, slots, rests))
 
 
 def by_roles(tensors, peers, heads, first, clips):

time: 127 us -> 134 us (1.055)
  starting transfers between devices: 20.2 us -> 54.3 us
  blocking collectives: 28 us -> 0 us
  waiting for transfers between devices: 57.1 us -> 55.3 us
    ppermute x10 -> x24, starting transfers between devices: 14.3 us -> 54.3 us  [swapped(): lax.ppermute(x, 'tm', [(i, i ^ by) for i in range(peers)])]
    all_to_all x1 -> x0, blocking collectives: 28 us -> none  [by_slots_and_columns(): back = lax.all_to_all(results, 'tm', 0, 0)]
    all_to_all x1 -> x0, waiting for transfers between devices: 10.1 us -> none  [by_slots_and_columns(): arrived = lax.all_to_all(packed, 'tm', 0, 0)]
    ppermute x10 -> x24, waiting for transfers between devices: 47 us -> 55.3 us  [swapped(): lax.ppermute(x, 'tm', [(i, i ^ by) for i in range(peers)])]
    all_to_all x1 -> x0, starting transfers between devices: 5.99 us -> none  [by_slots_and_columns(): arrived = lax.all_to_all(packed, 'tm', 0, 0)]
    pallas_call x3, Pallas kernels: 11.2 us -> 13.5 us  [the longest x1 7.53 us: slots_kernel(): pl.pallas_call(body, in_specs=[SMEM] * 3 + [VMEM] * blocks, out_specs=[VM...]
  transfers between devices with their start and end apart: 11 -> 24, of which waited for: 7 -> 8; matrix products, arithmetic and copies ran while one was open for 1% -> 2% of each run, Pallas kernels for 12% -> 11%
where the time goes in v1:
time: 134 us; the launch traced here: 133 us
  waiting for transfers between devices  55.3 us (41%)
  starting transfers between devices  54.3 us (41%)
  Pallas kernels  19.1 us (14%)
  other arithmetic  1.52 us (1%)
  between operations  1.41 us (1%)
    ppermute x24, waiting for transfers between devices, swapped(): lax.ppermute(x, 'tm', [(i, i ^ by) for i in range(peers)])  55.3 us
    ppermute x24, starting transfers between devices, swapped(): lax.ppermute(x, 'tm', [(i, i ^ by) for i in range(peers)])  54.3 us
    pallas_call x1, Pallas kernels, slots_kernel(): pl.pallas_call(body, in_specs=[SMEM] * 3 + [VMEM] * blocks, out_specs=[VM...  7.53 us
    pallas_call x1, Pallas kernels, slots_pack(): pl.pallas_call(body, in_specs=[SMEM] + [pl.BlockSpec(memory_space=pl.ANY)...  4.11 us
    pallas_call x1, Pallas kernels, rest_kernel(): pl.pallas_call(body, in_specs=[SMEM] * 3 + [VMEM] * (2 * columns), out_sp...  3.56 us
  transfers between devices with their start and end apart: 24, of which 8 were waited for; matrix products, arithmetic and copies ran while one was open for 2% of the time, Pallas kernels for 11%

profile of v1, /device:TPU:0, one launch (start us, length us, event | category | flops | bytes accessed | tf_op | source)
XLA Modules:
  0.0 132.9 jit_solution(13022009439208529598)
XLA Ops:
  0.6 2.1 %shard_map.87 = (bf16[5,128,128]{2,1,0:T(8,128)(2,1)}, bf16[5,128,128]{2,1,0:T(8,128)(2,1)}, bf16[5,128,128]{2,1,0:T(8,128)(2,1)}, bf16[5,128,128]{2,1,0:T(8,128)(2,1)}) custom-call(s32[1]{0:T(128)} %bitcast.column_ref, bf16[1,128,2560]{2,1,0:T(8,128)(2,1)} %refs_0_.3, bf16[1,128,2560]{2,1,0:T(8,128)(2,1)} %refs_1_.3, bf16[1,128,2560]{2,1,0:T(8,128)(2,1)} %refs_2_.3, ...), custom_call_target="tpu_custom_call" | custom-call | bytes 1310720 | tf_op jit(solution)/shard_map/pallas_call | solution.py:289
  2.7 3.1 %collective-permute-start = (bf16[5,128,128]{2,1,0:T(8,128)(2,1)}, bf16[5,128,128]{2,1,0:T(8,128)(2,1)S(1)}, u32[]{:S(2)}, u32[]{:S(2)}) collective-permute-start(bf16[5,128,128]{2,1,0:T(8,128)(2,1)} %get-tuple-element.71), channel_id=1, source_target_pairs={{0,8},{4,12},{8,0},{12,4},{16,24},{20,28},{24,16},{28,20},{1,9},{5... | collective-permute-start | bytes 491528 | tf_op jit(solution)/shard_map/ppermute | solution.py:364
  5.8 2.6 %collective-permute-start.1 = (bf16[5,128,128]{2,1,0:T(8,128)(2,1)}, bf16[5,128,128]{2,1,0:T(8,128)(2,1)S(1)}, u32[]{:S(2)}, u32[]{:S(2)}) collective-permute-start(bf16[5,128,128]{2,1,0:T(8,128)(2,1)} %get-tuple-element.72), channel_id=1, source_target_pairs={{0,16},{4,20},{8,24},{12,28},{16,0},{20,4},{24,8},{28,12},{1,17},{... | collective-permute-start | bytes 491528 | tf_op jit(solution)/shard_map/ppermute | solution.py:364
  8.4 0.0 collective-permute-start.2
  8.4 0.6 pad_add_fusion.where_ref
  9.0 0.0 copy-start.2
  9.0 4.1 %shard_map.86 = (bf16[10,128,128]{2,1,0:T(8,128)(2,1)}, bf16[10,128,128]{2,1,0:T(8,128)(2,1)}, bf16[10,128,128]{2,1,0:T(8,128)(2,1)}, bf16[10,128,128]{2,1,0:T(8...) custom-call(s32[3]{0:T(128)} %pad_add_fusion.where_ref, ...), custom_call_target="tpu_custom_call" | custom-call | bytes 5242880 | tf_op jit(solution)/shard_map/pallas_call | solution.py:261
  13.1 0.0 collective-permute-done.refs_1_
  13.1 8.0 %collective-permute-done.1.refs_2_ = bf16[5,128,128]{2,1,0:T(8,128)(2,1)S(1)} collective-permute-done((bf16[5,128,128]{2,1,0:T(8,128)(2,1)}, bf16[5,128,128]{2,1,0:T(8,128)(2,1)S(1)}, u32[]{:S(2)}, u32[]{:S(2)}) %collective-permute-start.1) | collective-permute-done | bytes 163872 | tf_op jit(solution)/shard_map/ppermute | solution.py:364
  21.1 0.0 collective-permute-done.2.refs_3_
  21.1 0.0 copy-done.2
  21.1 1.6 %collective-permute-start.10 = (bf16[5,128,128]{2,1,0:T(8,128)(2,1)S(1)}, bf16[5,128,128]{2,1,0:T(8,128)(2,1)S(1)}, u32[]{:S(2)}, u32[]{:S(2)}) collective-permute-start(bf16[5,128,128]{2,1,0:T(8,128)(2,1)S(1)} %copy-done.2), channel_id=1, source_target_pairs={{0,4},{4,0},{8,12},{12,8},{16,20},{20,16},{24,28},{28,24},{1,5},{5... | collective-permute-start | bytes 491528 | tf_op jit(solution)/shard_map/ppermute | solution.py:364
  22.7 0.5 collective-permute-start.3
  23.2 2.6 %collective-permute-start.4 = (bf16[10,128,128]{2,1,0:T(8,128)(2,1)}, bf16[10,128,128]{2,1,0:T(8,128)(2,1)S(1)}, u32[]{:S(2)}, u32[]{:S(2)}) collective-permute-start(bf16[10,128,128]{2,1,0:T(8,128)(2,1)} %get-tuple-element.76), channel_id=1, source_target_pairs={{0,8},{4,12},{8,0},{12,4},{16,24},{20,28},{24,16},{28,20},{1,9},{5... | collective-permute-start | bytes 983048 | tf_op jit(solution)/shard_map/ppermute | solution.py:364
  25.8 1.5 %collective-permute-start.11 = (bf16[5,128,128]{2,1,0:T(8,128)(2,1)S(1)}, bf16[5,128,128]{2,1,0:T(8,128)(2,1)S(1)}, u32[]{:S(2)}, u32[]{:S(2)}) collective-permute-start(bf16[5,128,128]{2,1,0:T(8,128)(2,1)S(1)} %collective-permute-done.refs_1_), channel_id=1, source_target_pairs={{0,4},{4,0},{8,12},{12,8},{16,20},{20,16},{24,28},{28,24},{1,5},{5... | collective-permute-start | bytes 491528 | tf_op jit(solution)/shard_map/ppermute | solution.py:364
  27.3 0.5 collective-permute-start.12
  27.8 0.5 collective-permute-done.10.refs_4_
  28.3 1.5 %collective-permute-start.13 = (bf16[5,128,128]{2,1,0:T(8,128)(2,1)S(1)}, bf16[5,128,128]{2,1,0:T(8,128)(2,1)S(1)}, u32[]{:S(2)}, u32[]{:S(2)}) collective-permute-start(bf16[5,128,128]{2,1,0:T(8,128)(2,1)S(1)} %collective-permute-done.2.refs_3_), channel_id=1, source_target_pairs={{0,4},{4,0},{8,12},{12,8},{16,20},{20,16},{24,28},{28,24},{1,5},{5... | collective-permute-start | bytes 491528 | tf_op jit(solution)/shard_map/ppermute | solution.py:364
  29.8 0.0 copy-done.3
  29.8 0.2 reduce-window.8
  30.0 0.1 select_reduce_fusion.1
  30.1 11.1 %collective-permute-done.11.refs_5_ = bf16[5,128,128]{2,1,0:T(8,128)(2,1)S(1)} collective-permute-done((bf16[5,128,128]{2,1,0:T(8,128)(2,1)S(1)}, bf16[5,128,128]{2,1,0:T(8,128)(2,1)S(1)}, u32[]{:S(2)}, u32[]{:S(2)}) %collective-permute-start.11) | collective-permute-done | bytes 163872 | tf_op jit(solution)/shard_map/ppermute | solution.py:364
  41.1 4.7 %collective-permute-start.5 = (bf16[10,128,128]{2,1,0:T(8,128)(2,1)}, bf16[10,128,128]{2,1,0:T(8,128)(2,1)S(1)}, u32[]{:S(2)}, u32[]{:S(2)}) collective-permute-start(bf16[10,128,128]{2,1,0:T(8,128)(2,1)} %get-tuple-element.77), channel_id=1, source_target_pairs={{0,12},{4,8},{8,4},{12,0},{16,28},{20,24},{24,20},{28,16},{1,13},{... | collective-permute-start | bytes 983048 | tf_op jit(solution)/shard_map/ppermute | solution.py:364
  45.9 0.0 collective-permute-done.12.refs_6_
  45.9 3.2 %collective-permute-start.6 = (bf16[10,128,128]{2,1,0:T(8,128)(2,1)}, bf16[10,128,128]{2,1,0:T(8,128)(2,1)S(1)}, u32[]{:S(2)}, u32[]{:S(2)}) collective-permute-start(bf16[10,128,128]{2,1,0:T(8,128)(2,1)} %get-tuple-element.78), channel_id=1, source_target_pairs={{0,16},{4,20},{8,24},{12,28},{16,0},{20,4},{24,8},{28,12},{1,17},{... | collective-permute-start | bytes 983048 | tf_op jit(solution)/shard_map/ppermute | solution.py:364
  49.0 0.0 collective-permute-done.13.refs_7_
  49.0 4.2 %collective-permute-start.7 = (bf16[10,128,128]{2,1,0:T(8,128)(2,1)}, bf16[10,128,128]{2,1,0:T(8,128)(2,1)S(1)}, u32[]{:S(2)}, u32[]{:S(2)}) collective-permute-start(bf16[10,128,128]{2,1,0:T(8,128)(2,1)} %get-tuple-element.79), channel_id=1, source_target_pairs={{0,20},{4,16},{8,28},{12,24},{16,4},{20,0},{24,12},{28,8},{1,21},{... | collective-permute-start | bytes 983048 | tf_op jit(solution)/shard_map/ppermute | solution.py:364
  53.2 0.0 collective-permute-done.3.refs_1_
  53.2 0.0 collective-permute-start.8
  53.2 0.0 collective-permute-done.4.refs_2_
  53.2 3.8 %collective-permute-start.9 = (bf16[10,128,128]{2,1,0:T(8,128)(2,1)}, bf16[10,128,128]{2,1,0:T(8,128)(2,1)S(1)}, u32[]{:S(2)}, u32[]{:S(2)}) collective-permute-start(bf16[10,128,128]{2,1,0:T(8,128)(2,1)} %get-tuple-element.81), channel_id=1, source_target_pairs={{0,28},{4,24},{8,20},{12,16},{16,12},{20,8},{24,4},{28,0},{1,29},{... | collective-permute-start | bytes 983048 | tf_op jit(solution)/shard_map/ppermute | solution.py:364
  57.0 0.6 fusion
  58.3 0.7 pad.2.clone
  59.0 0.1 add_add_fusion.clip_ref
  59.1 0.5 copy-done
  59.6 3.6 %shard_map.88 = (bf16[2,128,128]{2,1,0:T(8,128)(2,1)S(1)}, bf16[2,128,128]{2,1,0:T(8,128)(2,1)S(1)}, bf16[2,128,128]{2,1,0:T(8,128)(2,1)S(1)}, bf16[2,128,128]{2,1,0:T(8,128)(2,1)S(1)}) custom-call(s32[1]{0:T(128)S(6)} %copy.9.first_ref, s32[3,8]{1,0:T(4,128)S(1)} %add_add_fusion.clip_ref, s32[3]{0:T(128)S(1)} %copy-done, ...), custom_call_target="tpu_custom_call" | custom-call | flops 1073741824 | bytes 1835008 | tf_op jit(solution)/shard_map/pallas_call | solution.py:321
  63.2 0.0 collective-permute-done.5.refs_3_
  63.2 19.3 %collective-permute-done.6.refs_4_ = bf16[10,128,128]{2,1,0:T(8,128)(2,1)S(1)} collective-permute-done((bf16[10,128,128]{2,1,0:T(8,128)(2,1)}, bf16[10,128,128]{2,1,0:T(8,128)(2,1)S(1)}, u32[]{:S(2)}, u32[]{:S(2)}) %collective-permute-start.6) | collective-permute-done | bytes 327712 | tf_op jit(solution)/shard_map/ppermute | solution.py:364
  82.4 7.8 %collective-permute-done.7.refs_5_ = bf16[10,128,128]{2,1,0:T(8,128)(2,1)S(1)} collective-permute-done((bf16[10,128,128]{2,1,0:T(8,128)(2,1)}, bf16[10,128,128]{2,1,0:T(8,128)(2,1)S(1)}, u32[]{:S(2)}, u32[]{:S(2)}) %collective-permute-start.7) | collective-permute-done | bytes 327712 | tf_op jit(solution)/shard_map/ppermute | solution.py:364
  90.3 0.0 collective-permute-done.8.refs_6_
  90.3 0.0 collective-permute-done.9.refs_7_
  90.3 12.7 %collective-permute-start.14 = (bf16[2,128,128]{2,1,0:T(8,128)(2,1)S(1)}, bf16[2,128,128]{2,1,0:T(8,128)(2,1)S(1)}, u32[]{:S(2)}, u32[]{:S(2)}) collective-permute-start(bf16[2,128,128]{2,1,0:T(8,128)(2,1)S(1)} %get-tuple-element.107), channel_id=1, source_target_pairs={{0,8},{4,12},{8,0},{12,4},{16,24},{20,28},{24,16},{28,20},{1,9},{5... | collective-permute-start | bytes 196616 | tf_op jit(solution)/shard_map/ppermute | solution.py:364
  103.0 0.0 collective-permute-start.15
  103.0 2.4 %collective-permute-start.16 = (bf16[2,128,128]{2,1,0:T(8,128)(2,1)S(1)}, bf16[2,128,128]{2,1,0:T(8,128)(2,1)S(1)}, u32[]{:S(2)}, u32[]{:S(2)}) collective-permute-start(bf16[2,128,128]{2,1,0:T(8,128)(2,1)S(1)} %get-tuple-element.109), channel_id=1, source_target_pairs={{0,24},{4,28},{8,16},{12,20},{16,8},{20,12},{24,0},{28,4},{1,25},{... | collective-permute-start | bytes 196616 | tf_op jit(solution)/shard_map/ppermute | solution.py:364
  105.3 0.0 copy-done.1
  105.3 7.5 %shard_map.89 = (bf16[4,128,128]{2,1,0:T(8,128)(2,1)S(1)}, bf16[4,128,128]{2,1,0:T(8,128)(2,1)S(1)}, bf16[4,128,128]{2,1,0:T(8,128)(2,1)S(1)}, bf16[4,128,128]{2...) custom-call(s32[1]{0:T(128)S(6)} %copy.9.first_ref, ...), custom_call_target="tpu_custom_call" | custom-call | flops 2147483648 | bytes 3670016 | tf_op jit(solution)/shard_map/pallas_call | solution.py:232
  112.9 0.0 collective-permute-done.14.refs_9_
  112.9 0.0 collective-permute-done.15.refs_10_
  112.9 0.0 collective-permute-done.16.refs_11_
  112.9 0.1 collective-permute-start.17
  113.0 1.2 collective-permute-start.18
  114.2 2.3 %collective-permute-start.19 = (bf16[4,128,128]{2,1,0:T(8,128)(2,1)S(1)}, bf16[4,128,128]{2,1,0:T(8,128)(2,1)S(1)}, u32[]{:S(2)}, u32[]{:S(2)}) collective-permute-start(bf16[4,128,128]{2,1,0:T(8,128)(2,1)S(1)} %get-tuple-element.113), channel_id=1, source_target_pairs={{0,12},{4,8},{8,4},{12,0},{16,28},{20,24},{24,20},{28,16},{1,13},{... | collective-permute-start | bytes 393224 | tf_op jit(solution)/shard_map/ppermute | solution.py:364
  116.4 0.6 collective-permute-start.20
  117.0 1.9 %collective-permute-start.21 = (bf16[4,128,128]{2,1,0:T(8,128)(2,1)S(1)}, bf16[4,128,128]{2,1,0:T(8,128)(2,1)S(1)}, u32[]{:S(2)}, u32[]{:S(2)}) collective-permute-start(bf16[4,128,128]{2,1,0:T(8,128)(2,1)S(1)} %get-tuple-element.115), channel_id=1, source_target_pairs={{0,20},{4,16},{8,28},{12,24},{16,4},{20,0},{24,12},{28,8},{1,21},{... | collective-permute-start | bytes 393224 | tf_op jit(solution)/shard_map/ppermute | solution.py:364
  118.9 1.6 %collective-permute-done.17.refs_1_ = bf16[4,128,128]{2,1,0:T(8,128)(2,1)S(1)} collective-permute-done((bf16[4,128,128]{2,1,0:T(8,128)(2,1)S(1)}, bf16[4,128,128]{2,1,0:T(8,128)(2,1)S(1)}, u32[]{:S(2)}, u32[]{:S(2)}) %collective-permute-start.17) | collective-permute-done | bytes 131104 | tf_op jit(solution)/shard_map/ppermute | solution.py:364
  120.5 1.6 %collective-permute-start.22 = (bf16[4,128,128]{2,1,0:T(8,128)(2,1)S(1)}, bf16[4,128,128]{2,1,0:T(8,128)(2,1)S(1)}, u32[]{:S(2)}, u32[]{:S(2)}) collective-permute-start(bf16[4,128,128]{2,1,0:T(8,128)(2,1)S(1)} %get-tuple-element.116), channel_id=1, source_target_pairs={{0,24},{4,28},{8,16},{12,20},{16,8},{20,12},{24,0},{28,4},{1,25},{... | collective-permute-start | bytes 393224 | tf_op jit(solution)/shard_map/ppermute | solution.py:364
  122.1 0.0 collective-permute-done.18.refs_2_
  122.1 2.0 %collective-permute-start.23 = (bf16[4,128,128]{2,1,0:T(8,128)(2,1)S(1)}, bf16[4,128,128]{2,1,0:T(8,128)(2,1)S(1)}, u32[]{:S(2)}, u32[]{:S(2)}) collective-permute-start(bf16[4,128,128]{2,1,0:T(8,128)(2,1)S(1)} %get-tuple-element.117), channel_id=1, source_target_pairs={{0,28},{4,24},{8,20},{12,16},{16,12},{20,8},{24,4},{28,0},{1,29},{... | collective-permute-start | bytes 393224 | tf_op jit(solution)/shard_map/ppermute | solution.py:364
  124.1 0.0 collective-permute-done.19.refs_3_
  124.1 5.3 %collective-permute-done.20.refs_4_ = bf16[4,128,128]{2,1,0:T(8,128)(2,1)S(1)} collective-permute-done((bf16[4,128,128]{2,1,0:T(8,128)(2,1)S(1)}, bf16[4,128,128]{2,1,0:T(8,128)(2,1)S(1)}, u32[]{:S(2)}, u32[]{:S(2)}) %collective-permute-start.20) | collective-permute-done | bytes 131104 | tf_op jit(solution)/shard_map/ppermute | solution.py:364
  129.4 1.7 %collective-permute-done.21.refs_5_ = bf16[4,128,128]{2,1,0:T(8,128)(2,1)S(1)} collective-permute-done((bf16[4,128,128]{2,1,0:T(8,128)(2,1)S(1)}, bf16[4,128,128]{2,1,0:T(8,128)(2,1)S(1)}, u32[]{:S(2)}, u32[]{:S(2)}) %collective-permute-start.21) | collective-permute-done | bytes 131104 | tf_op jit(solution)/shard_map/ppermute | solution.py:364
  131.1 0.0 collective-permute-done.22.refs_6_
  131.1 0.0 collective-permute-done.23.refs_7_
  131.1 1.8 %shard_map.90 = (bf16[1,128,2560]{2,1,0:T(8,128)(2,1)}, bf16[1,128,2560]{2,1,0:T(8,128)(2,1)}) custom-call(s32[3]{0:T(128)S(1)} %copy-done, bf16[4,128,128]{2,1,0:T(8,128)(2,1)S(1)} %get-tuple-element.110.refs_0_, bf16[4,128,128]{2,1,0:T(8,128)(2,1)S(1)} %collective-permute-done.17.refs_1_, bf16[4,128,128]{2,1,0:T(8,128)(2,1)S(1)} %collective-permute-done.18.refs_2_, ...), custom_call_target="tpu_custom_call" | custom-call | bytes 2621440 | tf_op jit(solution)/shard_map/pallas_call | solution.py:349
  (3 shorter events, 0.0 us)
Async XLA Ops:
  2.7 10.4 %collective-permute-start = (bf16[5,128,128]{2,1,0:T(8,128)(2,1)}, bf16[5,128,128]{2,1,0:T(8,128)(2,1)S(1)}, u32[]{:S(2)}, u32[]{:S(2)}) collective-permute-start(bf16[5,128,128]{2,1,0:T(8,128)(2,1)} %get-tuple-element.71), channel_id=1, source_target_pairs={{0,8},{4,12},{8,0},{12,4},{16,24},{20,28},{24,16},{28,20},{1,9},{5... | collective-permute-start | bytes 491528 | tf_op jit(solution)/shard_map/ppermute | solution.py:364
  5.8 15.3 %collective-permute-start.1 = (bf16[5,128,128]{2,1,0:T(8,128)(2,1)}, bf16[5,128,128]{2,1,0:T(8,128)(2,1)S(1)}, u32[]{:S(2)}, u32[]{:S(2)}) collective-permute-start(bf16[5,128,128]{2,1,0:T(8,128)(2,1)} %get-tuple-element.72), channel_id=1, source_target_pairs={{0,16},{4,20},{8,24},{12,28},{16,0},{20,4},{24,8},{28,12},{1,17},{... | collective-permute-start | bytes 491528 | tf_op jit(solution)/shard_map/ppermute | solution.py:364
  8.4 12.7 %collective-permute-start.2 = (bf16[5,128,128]{2,1,0:T(8,128)(2,1)}, bf16[5,128,128]{2,1,0:T(8,128)(2,1)S(1)}, u32[]{:S(2)}, u32[]{:S(2)}) collective-permute-start(bf16[5,128,128]{2,1,0:T(8,128)(2,1)} %get-tuple-element.73), channel_id=1, source_target_pairs={{0,24},{4,28},{8,16},{12,20},{16,8},{20,12},{24,0},{28,4},{1,25},{... | collective-permute-start | bytes 491528 | tf_op jit(solution)/shard_map/ppermute | solution.py:364
  9.0 12.1 %copy-start.2 = (bf16[5,128,128]{2,1,0:T(8,128)(2,1)S(1)}, bf16[5,128,128]{2,1,0:T(8,128)(2,1)}, u32[]{:S(2)}) copy-start(bf16[5,128,128]{2,1,0:T(8,128)(2,1)} %get-tuple-element.82.refs_0_) | copy-start | bytes 491524
  21.1 8.7 %copy-start.3 = (s32[1,3]{1,0:T(1,128)S(1)}, s32[1,3]{1,0:T(1,128)}, u32[]{:S(2)}) copy-start(s32[1,3]{1,0:T(1,128)} %param.13) | copy-start | bytes 40
  21.1 7.2 %collective-permute-start.10 = (bf16[5,128,128]{2,1,0:T(8,128)(2,1)S(1)}, bf16[5,128,128]{2,1,0:T(8,128)(2,1)S(1)}, u32[]{:S(2)}, u32[]{:S(2)}) collective-permute-start(bf16[5,128,128]{2,1,0:T(8,128)(2,1)S(1)} %copy-done.2), channel_id=1, source_target_pairs={{0,4},{4,0},{8,12},{12,8},{16,20},{20,16},{24,28},{28,24},{1,5},{5... | collective-permute-start | bytes 491528 | tf_op jit(solution)/shard_map/ppermute | solution.py:364
  22.7 30.6 %collective-permute-start.3 = (bf16[10,128,128]{2,1,0:T(8,128)(2,1)}, bf16[10,128,128]{2,1,0:T(8,128)(2,1)S(1)}, u32[]{:S(2)}, u32[]{:S(2)}) collective-permute-start(bf16[10,128,128]{2,1,0:T(8,128)(2,1)} %get-tuple-element.75), channel_id=1, source_target_pairs={{0,4},{4,0},{8,12},{12,8},{16,20},{20,16},{24,28},{28,24},{1,5},{5... | collective-permute-start | bytes 983048 | tf_op jit(solution)/shard_map/ppermute | solution.py:364
  23.2 30.0 %collective-permute-start.4 = (bf16[10,128,128]{2,1,0:T(8,128)(2,1)}, bf16[10,128,128]{2,1,0:T(8,128)(2,1)S(1)}, u32[]{:S(2)}, u32[]{:S(2)}) collective-permute-start(bf16[10,128,128]{2,1,0:T(8,128)(2,1)} %get-tuple-element.76), channel_id=1, source_target_pairs={{0,8},{4,12},{8,0},{12,4},{16,24},{20,28},{24,16},{28,20},{1,9},{5... | collective-permute-start | bytes 983048 | tf_op jit(solution)/shard_map/ppermute | solution.py:364
  25.8 15.4 %collective-permute-start.11 = (bf16[5,128,128]{2,1,0:T(8,128)(2,1)S(1)}, bf16[5,128,128]{2,1,0:T(8,128)(2,1)S(1)}, u32[]{:S(2)}, u32[]{:S(2)}) collective-permute-start(bf16[5,128,128]{2,1,0:T(8,128)(2,1)S(1)} %collective-permute-done.refs_1_), channel_id=1, source_target_pairs={{0,4},{4,0},{8,12},{12,8},{16,20},{20,16},{24,28},{28,24},{1,5},{5... | collective-permute-start | bytes 491528 | tf_op jit(solution)/shard_map/ppermute | solution.py:364
  27.3 18.6 %collective-permute-start.12 = (bf16[5,128,128]{2,1,0:T(8,128)(2,1)S(1)}, bf16[5,128,128]{2,1,0:T(8,128)(2,1)S(1)}, u32[]{:S(2)}, u32[]{:S(2)}) collective-permute-start(bf16[5,128,128]{2,1,0:T(8,128)(2,1)S(1)} %collective-permute-done.1.refs_2_), channel_id=1, source_target_pairs={{0,4},{4,0},{8,12},{12,8},{16,20},{20,16},{24,28},{28,24},{1,5},{5... | collective-permute-start | bytes 491528 | tf_op jit(solution)/shard_map/ppermute | solution.py:364
  28.3 20.7 %collective-permute-start.13 = (bf16[5,128,128]{2,1,0:T(8,128)(2,1)S(1)}, bf16[5,128,128]{2,1,0:T(8,128)(2,1)S(1)}, u32[]{:S(2)}, u32[]{:S(2)}) collective-permute-start(bf16[5,128,128]{2,1,0:T(8,128)(2,1)S(1)} %collective-permute-done.2.refs_3_), channel_id=1, source_target_pairs={{0,4},{4,0},{8,12},{12,8},{16,20},{20,16},{24,28},{28,24},{1,5},{5... | collective-permute-start | bytes 491528 | tf_op jit(solution)/shard_map/ppermute | solution.py:364
  41.1 22.1 %collective-permute-start.5 = (bf16[10,128,128]{2,1,0:T(8,128)(2,1)}, bf16[10,128,128]{2,1,0:T(8,128)(2,1)S(1)}, u32[]{:S(2)}, u32[]{:S(2)}) collective-permute-start(bf16[10,128,128]{2,1,0:T(8,128)(2,1)} %get-tuple-element.77), channel_id=1, source_target_pairs={{0,12},{4,8},{8,4},{12,0},{16,28},{20,24},{24,20},{28,16},{1,13},{... | collective-permute-start | bytes 983048 | tf_op jit(solution)/shard_map/ppermute | solution.py:364
  45.9 36.6 %collective-permute-start.6 = (bf16[10,128,128]{2,1,0:T(8,128)(2,1)}, bf16[10,128,128]{2,1,0:T(8,128)(2,1)S(1)}, u32[]{:S(2)}, u32[]{:S(2)}) collective-permute-start(bf16[10,128,128]{2,1,0:T(8,128)(2,1)} %get-tuple-element.78), channel_id=1, source_target_pairs={{0,16},{4,20},{8,24},{12,28},{16,0},{20,4},{24,8},{28,12},{1,17},{... | collective-permute-start | bytes 983048 | tf_op jit(solution)/shard_map/ppermute | solution.py:364
  49.0 41.2 %collective-permute-start.7 = (bf16[10,128,128]{2,1,0:T(8,128)(2,1)}, bf16[10,128,128]{2,1,0:T(8,128)(2,1)S(1)}, u32[]{:S(2)}, u32[]{:S(2)}) collective-permute-start(bf16[10,128,128]{2,1,0:T(8,128)(2,1)} %get-tuple-element.79), channel_id=1, source_target_pairs={{0,20},{4,16},{8,28},{12,24},{16,4},{20,0},{24,12},{28,8},{1,21},{... | collective-permute-start | bytes 983048 | tf_op jit(solution)/shard_map/ppermute | solution.py:364
  53.2 37.1 %collective-permute-start.8 = (bf16[10,128,128]{2,1,0:T(8,128)(2,1)}, bf16[10,128,128]{2,1,0:T(8,128)(2,1)S(1)}, u32[]{:S(2)}, u32[]{:S(2)}) collective-permute-start(bf16[10,128,128]{2,1,0:T(8,128)(2,1)} %get-tuple-element.80), channel_id=1, source_target_pairs={{0,24},{4,28},{8,16},{12,20},{16,8},{20,12},{24,0},{28,4},{1,25},{... | collective-permute-start | bytes 983048 | tf_op jit(solution)/shard_map/ppermute | solution.py:364
  53.2 37.0 %collective-permute-start.9 = (bf16[10,128,128]{2,1,0:T(8,128)(2,1)}, bf16[10,128,128]{2,1,0:T(8,128)(2,1)S(1)}, u32[]{:S(2)}, u32[]{:S(2)}) collective-permute-start(bf16[10,128,128]{2,1,0:T(8,128)(2,1)} %get-tuple-element.81), channel_id=1, source_target_pairs={{0,28},{4,24},{8,20},{12,16},{16,12},{20,8},{24,4},{28,0},{1,29},{... | collective-permute-start | bytes 983048 | tf_op jit(solution)/shard_map/ppermute | solution.py:364
  59.0 0.6 copy-start
  59.6 45.7 %copy-start.1 = (bf16[10,128,128]{2,1,0:T(8,128)(2,1)S(1)}, bf16[10,128,128]{2,1,0:T(8,128)(2,1)}, u32[]{:S(2)}) copy-start(bf16[10,128,128]{2,1,0:T(8,128)(2,1)} %get-tuple-element.90.refs_0_) | copy-start | bytes 983044
  90.3 22.6 %collective-permute-start.14 = (bf16[2,128,128]{2,1,0:T(8,128)(2,1)S(1)}, bf16[2,128,128]{2,1,0:T(8,128)(2,1)S(1)}, u32[]{:S(2)}, u32[]{:S(2)}) collective-permute-start(bf16[2,128,128]{2,1,0:T(8,128)(2,1)S(1)} %get-tuple-element.107), channel_id=1, source_target_pairs={{0,8},{4,12},{8,0},{12,4},{16,24},{20,28},{24,16},{28,20},{1,9},{5... | collective-permute-start | bytes 196616 | tf_op jit(solution)/shard_map/ppermute | solution.py:364
  103.0 9.9 %collective-permute-start.15 = (bf16[2,128,128]{2,1,0:T(8,128)(2,1)S(1)}, bf16[2,128,128]{2,1,0:T(8,128)(2,1)S(1)}, u32[]{:S(2)}, u32[]{:S(2)}) collective-permute-start(bf16[2,128,128]{2,1,0:T(8,128)(2,1)S(1)} %get-tuple-element.108), channel_id=1, source_target_pairs={{0,16},{4,20},{8,24},{12,28},{16,0},{20,4},{24,8},{28,12},{1,17},{... | collective-permute-start | bytes 196616 | tf_op jit(solution)/shard_map/ppermute | solution.py:364
  103.0 9.9 %collective-permute-start.16 = (bf16[2,128,128]{2,1,0:T(8,128)(2,1)S(1)}, bf16[2,128,128]{2,1,0:T(8,128)(2,1)S(1)}, u32[]{:S(2)}, u32[]{:S(2)}) collective-permute-start(bf16[2,128,128]{2,1,0:T(8,128)(2,1)S(1)} %get-tuple-element.109), channel_id=1, source_target_pairs={{0,24},{4,28},{8,16},{12,20},{16,8},{20,12},{24,0},{28,4},{1,25},{... | collective-permute-start | bytes 196616 | tf_op jit(solution)/shard_map/ppermute | solution.py:364
  112.9 7.6 %collective-permute-start.17 = (bf16[4,128,128]{2,1,0:T(8,128)(2,1)S(1)}, bf16[4,128,128]{2,1,0:T(8,128)(2,1)S(1)}, u32[]{:S(2)}, u32[]{:S(2)}) collective-permute-start(bf16[4,128,128]{2,1,0:T(8,128)(2,1)S(1)} %get-tuple-element.111), channel_id=1, source_target_pairs={{0,4},{4,0},{8,12},{12,8},{16,20},{20,16},{24,28},{28,24},{1,5},{5... | collective-permute-start | bytes 393224 | tf_op jit(solution)/shard_map/ppermute | solution.py:364
  113.0 9.1 %collective-permute-start.18 = (bf16[4,128,128]{2,1,0:T(8,128)(2,1)S(1)}, bf16[4,128,128]{2,1,0:T(8,128)(2,1)S(1)}, u32[]{:S(2)}, u32[]{:S(2)}) collective-permute-start(bf16[4,128,128]{2,1,0:T(8,128)(2,1)S(1)} %get-tuple-element.112), channel_id=1, source_target_pairs={{0,8},{4,12},{8,0},{12,4},{16,24},{20,28},{24,16},{28,20},{1,9},{5... | collective-permute-start | bytes 393224 | tf_op jit(solution)/shard_map/ppermute | solution.py:364
  114.2 9.9 %collective-permute-start.19 = (bf16[4,128,128]{2,1,0:T(8,128)(2,1)S(1)}, bf16[4,128,128]{2,1,0:T(8,128)(2,1)S(1)}, u32[]{:S(2)}, u32[]{:S(2)}) collective-permute-start(bf16[4,128,128]{2,1,0:T(8,128)(2,1)S(1)} %get-tuple-element.113), channel_id=1, source_target_pairs={{0,12},{4,8},{8,4},{12,0},{16,28},{20,24},{24,20},{28,16},{1,13},{... | collective-permute-start | bytes 393224 | tf_op jit(solution)/shard_map/ppermute | solution.py:364
  116.4 12.9 %collective-permute-start.20 = (bf16[4,128,128]{2,1,0:T(8,128)(2,1)S(1)}, bf16[4,128,128]{2,1,0:T(8,128)(2,1)S(1)}, u32[]{:S(2)}, u32[]{:S(2)}) collective-permute-start(bf16[4,128,128]{2,1,0:T(8,128)(2,1)S(1)} %get-tuple-element.114), channel_id=1, source_target_pairs={{0,16},{4,20},{8,24},{12,28},{16,0},{20,4},{24,8},{28,12},{1,17},{... | collective-permute-start | bytes 393224 | tf_op jit(solution)/shard_map/ppermute | solution.py:364
  117.0 14.0 %collective-permute-start.21 = (bf16[4,128,128]{2,1,0:T(8,128)(2,1)S(1)}, bf16[4,128,128]{2,1,0:T(8,128)(2,1)S(1)}, u32[]{:S(2)}, u32[]{:S(2)}) collective-permute-start(bf16[4,128,128]{2,1,0:T(8,128)(2,1)S(1)} %get-tuple-element.115), channel_id=1, source_target_pairs={{0,20},{4,16},{8,28},{12,24},{16,4},{20,0},{24,12},{28,8},{1,21},{... | collective-permute-start | bytes 393224 | tf_op jit(solution)/shard_map/ppermute | solution.py:364
  120.5 10.5 %collective-permute-start.22 = (bf16[4,128,128]{2,1,0:T(8,128)(2,1)S(1)}, bf16[4,128,128]{2,1,0:T(8,128)(2,1)S(1)}, u32[]{:S(2)}, u32[]{:S(2)}) collective-permute-start(bf16[4,128,128]{2,1,0:T(8,128)(2,1)S(1)} %get-tuple-element.116), channel_id=1, source_target_pairs={{0,24},{4,28},{8,16},{12,20},{16,8},{20,12},{24,0},{28,4},{1,25},{... | collective-permute-start | bytes 393224 | tf_op jit(solution)/shard_map/ppermute | solution.py:364
  122.1 8.9 %collective-permute-start.23 = (bf16[4,128,128]{2,1,0:T(8,128)(2,1)S(1)}, bf16[4,128,128]{2,1,0:T(8,128)(2,1)S(1)}, u32[]{:S(2)}, u32[]{:S(2)}) collective-permute-start(bf16[4,128,128]{2,1,0:T(8,128)(2,1)S(1)} %get-tuple-element.117), channel_id=1, source_target_pairs={{0,28},{4,24},{8,20},{12,16},{16,12},{20,8},{24,4},{28,0},{1,29},{... | collective-permute-start | bytes 393224 | tf_op jit(solution)/shard_map/ppermute | solution.py:364

commit v2 on v1

--- a/solution.py
+++ b/solution.py
@@ -213,11 +213,9 @@
 
 
 def slots_kernel(full, blocks, first, clips, where, arrived):
-    def body(first_ref, clip_ref, where_ref, *refs):
-        x_refs, o_refs, (x, y) = refs[:blocks], refs[blocks : 2 * blocks], refs[2 * blocks :]
+    def body(first_ref, clip_ref, where_ref, x, *refs):
+        o_refs, y = refs[:blocks], refs[blocks]
         at = [where_ref[2] ^ d for d in range(blocks)]
-        for d in range(blocks):
-            x[at[d]] = x_refs[d][...]
 
         def head(s, carry):
             sources = [(x, 5 * s + t) for t in range(5)]
@@ -231,45 +229,13 @@
 
     return pl.pallas_call(
         body,
-        in_specs=[SMEM] * 3 + [VMEM] * blocks,
+        in_specs=[SMEM] * 3 + [VMEM],
         out_specs=[VMEM] * blocks,
         out_shape=[jax.ShapeDtypeStruct((2 * full, TOK, HD), jnp.bfloat16)] * blocks,
-        scratch_shapes=[
-            pltpu.VMEM((blocks, 5 * full, TOK, HD), jnp.bfloat16),
-            pltpu.VMEM((blocks, 2 * full, TOK, HD), jnp.bfloat16),
-        ],
+        scratch_shapes=[pltpu.VMEM((blocks, 2 * full, TOK, HD), jnp.bfloat16)],
         compiler_params=LOCAL,
         cost_estimate=cost(2 * full, blocks, 7 * full),
-    )(first, clips, where, *arrived)
-
-
-def slots_pack(full, peers, where, tensors):
-    def body(where_ref, *refs):
-        o_refs, (rows, sems) = refs[5 : 5 + peers], refs[5 + peers :]
-        copies = []
-        for t in range(5):
-            source = refs[t].at[0, :, pl.ds(0, full * peers * HD)]
-            copies.append(pltpu.make_async_copy(source, rows.at[t], sems.at[t]))
-            copies[-1].start()
-        for t in range(5):
-            copies[t].wait()
-            for s in range(full):
-                for d in range(peers):
-                    at = pl.multiple_of((s * peers + (where_ref[2] ^ d)) * HD, HD)
-                    o_refs[d][5 * s + t] = rows[t, :, pl.ds(at, HD)]
-
-    return pl.pallas_call(
-        body,
-        in_specs=[SMEM] + [pl.BlockSpec(memory_space=pl.ANY)] * 5,
-        out_specs=[VMEM] * peers,
-        out_shape=[jax.ShapeDtypeStruct((5 * full, TOK, HD), jnp.bfloat16)] * peers,
-        scratch_shapes=[
-            pltpu.VMEM((5, TOK, full * peers * HD), jnp.bfloat16),
-            pltpu.SemaphoreType.DMA((5,)),
-        ],
-        compiler_params=WHOLE,
-        cost_estimate=cost(0, peers, 10 * full),
-    )(where, *tensors)
+    )(first, clips, where, arrived)
 
 
 def rest_pack(base, columns, column, tensors):
@@ -365,9 +331,10 @@
 
     pieces = rest_pack(full * peers, rest, where[:1], tensors)
     own = [swapped(x, 2 * s) for s, x in enumerate(pieces)]
-    packed = slots_pack(full, peers, where, tensors)
+    plan = [[(t, s * peers + p) for s in range(full) for t in range(5)] for p in range(peers)]
+    packed = pack(plan, [(s * peers, peers) for s in range(full)], tensors)
     packed, own = lax.optimization_barrier((packed, own))
-    arrived = [swapped(x, d) for d, x in enumerate(packed)]
+    arrived = lax.all_to_all(packed, "tm", 0, 0)
     other = [swapped(x, 1) for x in own]
     pieces = rest_kernel(rest, first, clips, where, own, other)
     arrived, pieces = lax.optimization_barrier((arrived, pieces))

time: 134 us -> 125 us (0.933)
  starting transfers between devices: 54.3 us -> 31.8 us
  waiting for transfers between devices: 55.3 us -> 69.5 us
  local copies, waits for them, and re-layouts: 1.23 us -> 2.59 us
    ppermute x24 -> x17, starting transfers between devices: 54.3 us -> 25.8 us  [swapped(): lax.ppermute(x, 'tm', [(i, i ^ by) for i in range(peers)])]
    all_to_all x0 -> x1, waiting for transfers between devices: none -> 8.89 us  [by_slots_and_columns(): arrived = lax.all_to_all(packed, 'tm', 0, 0)]
    all_to_all x0 -> x1, starting transfers between devices: none -> 5.99 us  [by_slots_and_columns(): arrived = lax.all_to_all(packed, 'tm', 0, 0)]
    ppermute x24 -> x17, waiting for transfers between devices: 55.3 us -> 60.6 us  [swapped(): lax.ppermute(x, 'tm', [(i, i ^ by) for i in range(peers)])]
    pallas_call x2, Pallas kernels: 11.6 us -> 10.1 us  [the longest x1 7.39 us: slots_kernel(): pl.pallas_call(body, in_specs=[SMEM] * 3 + [VMEM], out_specs=[VMEM] * blo...]
    unnamed x8 -> x10, local copies, waits for them, and re-layouts: 0.51 us -> 1.87 us
  transfers between devices with their start and end apart: 24 -> 18, of which waited for: 8 -> 10; matrix products, arithmetic and copies ran while one was open for 2% -> 1% of each run, Pallas kernels for 11% -> 11%
where the time goes in v2:
time: 125 us; the launch traced here: 124 us
  waiting for transfers between devices  69.5 us (56%)
  starting transfers between devices  31.8 us (25%)
  Pallas kernels  18.1 us (14%)
  local copies, waits for them, and re-layouts  2.59 us (2%)
  between operations  1.39 us (1%)
    ppermute x17, waiting for transfers between devices, swapped(): lax.ppermute(x, 'tm', [(i, i ^ by) for i in range(peers)])  60.6 us
    ppermute x17, starting transfers between devices, swapped(): lax.ppermute(x, 'tm', [(i, i ^ by) for i in range(peers)])  25.8 us
    all_to_all x1, waiting for transfers between devices, by_slots_and_columns(): arrived = lax.all_to_all(packed, 'tm', 0, 0)  8.89 us
    pallas_call x1, Pallas kernels, slots_kernel(): pl.pallas_call(body, in_specs=[SMEM] * 3 + [VMEM], out_specs=[VMEM] * blo...  7.39 us
    all_to_all x1, starting transfers between devices, by_slots_and_columns(): arrived = lax.all_to_all(packed, 'tm', 0, 0)  5.99 us
    pallas_call x1, Pallas kernels, rest_kernel(): pl.pallas_call(body, in_specs=[SMEM] * 3 + [VMEM] * (2 * columns), out_sp...  4.11 us
    pallas_call x1, Pallas kernels, pack(): pl.pallas_call(body, in_specs=[pl.BlockSpec(memory_space=pl.ANY)] * len(t...  2.7 us
  transfers between devices with their start and end apart: 18, of which 10 were waited for; matrix products, arithmetic and copies ran while one was open for 1% of the time, Pallas kernels for 11%

profile of v2, /device:TPU:0, one launch (start us, length us, event | category | flops | bytes accessed | tf_op | source)
XLA Modules:
  0.0 124.5 jit_solution(776967045824634457)
XLA Ops:
  0.6 2.1 %shard_map.87 = (bf16[5,128,128]{2,1,0:T(8,128)(2,1)}, bf16[5,128,128]{2,1,0:T(8,128)(2,1)}, bf16[5,128,128]{2,1,0:T(8,128)(2,1)}, bf16[5,128,128]{2,1,0:T(8,128)(2,1)}) custom-call(s32[1]{0:T(128)} %bitcast.column_ref, bf16[1,128,2560]{2,1,0:T(8,128)(2,1)} %refs_0_.3, bf16[1,128,2560]{2,1,0:T(8,128)(2,1)} %refs_1_.3, bf16[1,128,2560]{2,1,0:T(8,128)(2,1)} %refs_2_.3, ...), custom_call_target="tpu_custom_call" | custom-call | bytes 1310720 | tf_op jit(solution)/shard_map/pallas_call | solution.py:255
  2.7 3.1 %collective-permute-start = (bf16[5,128,128]{2,1,0:T(8,128)(2,1)}, bf16[5,128,128]{2,1,0:T(8,128)(2,1)S(1)}, u32[]{:S(2)}, u32[]{:S(2)}) collective-permute-start(bf16[5,128,128]{2,1,0:T(8,128)(2,1)} %get-tuple-element.41), channel_id=1, source_target_pairs={{0,8},{4,12},{8,0},{12,4},{16,24},{20,28},{24,16},{28,20},{1,9},{5... | collective-permute-start | bytes 491528 | tf_op jit(solution)/shard_map/ppermute | solution.py:330
  5.8 2.6 %collective-permute-start.1 = (bf16[5,128,128]{2,1,0:T(8,128)(2,1)}, bf16[5,128,128]{2,1,0:T(8,128)(2,1)S(1)}, u32[]{:S(2)}, u32[]{:S(2)}) collective-permute-start(bf16[5,128,128]{2,1,0:T(8,128)(2,1)} %get-tuple-element.42), channel_id=1, source_target_pairs={{0,16},{4,20},{8,24},{12,28},{16,0},{20,4},{24,8},{28,12},{1,17},{... | collective-permute-start | bytes 491528 | tf_op jit(solution)/shard_map/ppermute | solution.py:330
  8.4 0.0 collective-permute-start.2
  8.4 2.7 %shard_map.86 = bf16[8,10,128,128]{3,2,1,0:T(8,128)(2,1)} custom-call(bf16[1,128,2560]{2,1,0:T(8,128)(2,1)} %refs_0_.3, bf16[1,128,2560]{2,1,0:T(8,128)(2,1)} %refs_1_.3, bf16[1,128,2560]{2,1,0:T(8,128)(2,1)} %refs_2_.3, bf16[1,128,2560]{2,1,0:T(8,128)(2,1)} %refs_3_.3, bf16[1,128,2560]{2,1,0:T(8,128)(2,1)} %refs_4_.3), custom_call_target="tpu_custom_call" | custom-call | bytes 5242880 | tf_op jit(solution)/shard_map/pallas_call | solution.py:144
  11.1 1.6 %collective-permute-done.refs_1_ = bf16[5,128,128]{2,1,0:T(8,128)(2,1)S(1)} collective-permute-done((bf16[5,128,128]{2,1,0:T(8,128)(2,1)}, bf16[5,128,128]{2,1,0:T(8,128)(2,1)S(1)}, u32[]{:S(2)}, u32[]{:S(2)}) %collective-permute-start) | collective-permute-done | bytes 163872 | tf_op jit(solution)/shard_map/ppermute | solution.py:330
  12.7 8.4 %collective-permute-done.1.refs_2_ = bf16[5,128,128]{2,1,0:T(8,128)(2,1)S(1)} collective-permute-done((bf16[5,128,128]{2,1,0:T(8,128)(2,1)}, bf16[5,128,128]{2,1,0:T(8,128)(2,1)S(1)}, u32[]{:S(2)}, u32[]{:S(2)}) %collective-permute-start.1) | collective-permute-done | bytes 163872 | tf_op jit(solution)/shard_map/ppermute | solution.py:330
  21.1 0.0 collective-permute-done.2.refs_3_
  21.1 0.0 copy-start.4
  21.1 0.0 copy-start
  21.1 6.0 %all-to-all-start = ((bf16[8,10,128,128]{3,2,1,0:T(8,128)(2,1)}), bf16[8,10,128,128]{3,2,1,0:T(8,128)(2,1)S(1)}, u32[]{:S(2)}, u32[]{:S(2)}) async-start(bf16[8,10,128,128]{3,2,1,0:T(8,128)(2,1)} %shard_map.86), calls=%async_computation | async-start | bytes 5242880 | tf_op jit(solution)/shard_map/all_to_all | solution.py:337
  27.1 0.0 copy-done.4
  27.1 0.2 reduce-window.8
  27.3 0.6 fusion
  27.9 0.7 pad.2.clone
  28.6 0.1 select_reduce_fusion.1
  28.7 0.0 copy-done
  28.7 2.1 %collective-permute-start.3 = (bf16[5,128,128]{2,1,0:T(8,128)(2,1)S(1)}, bf16[5,128,128]{2,1,0:T(8,128)(2,1)S(1)}, u32[]{:S(2)}, u32[]{:S(2)}) collective-permute-start(bf16[5,128,128]{2,1,0:T(8,128)(2,1)S(1)} %copy-done), channel_id=1, source_target_pairs={{0,4},{4,0},{8,12},{12,8},{16,20},{20,16},{24,28},{28,24},{1,5},{5... | collective-permute-start | bytes 491528 | tf_op jit(solution)/shard_map/ppermute | solution.py:330
  30.8 0.1 collective-permute-start.4
  30.9 1.9 %collective-permute-start.5 = (bf16[5,128,128]{2,1,0:T(8,128)(2,1)S(1)}, bf16[5,128,128]{2,1,0:T(8,128)(2,1)}, u32[]{:S(2)}, u32[]{:S(2)}) collective-permute-start(bf16[5,128,128]{2,1,0:T(8,128)(2,1)S(1)} %collective-permute-done.1.refs_2_), channel_id=1, source_target_pairs={{0,4},{4,0},{8,12},{12,8},{16,20},{20,16},{24,28},{28,24},{1,5},{5... | collective-permute-start | bytes 491528 | tf_op jit(solution)/shard_map/ppermute | solution.py:330
  32.8 0.1 collective-permute-start.6
  32.9 0.1 add_add_fusion.clip_ref
  33.6 0.1 pad_add_fusion.where_ref
  33.7 20.2 %collective-permute-done.3.refs_4_ = bf16[5,128,128]{2,1,0:T(8,128)(2,1)S(1)} collective-permute-done((bf16[5,128,128]{2,1,0:T(8,128)(2,1)S(1)}, bf16[5,128,128]{2,1,0:T(8,128)(2,1)S(1)}, u32[]{:S(2)}, u32[]{:S(2)}) %collective-permute-start.3) | collective-permute-done | bytes 163872 | tf_op jit(solution)/shard_map/ppermute | solution.py:330
  53.9 6.3 %collective-permute-done.4.refs_5_ = bf16[5,128,128]{2,1,0:T(8,128)(2,1)} collective-permute-done((bf16[5,128,128]{2,1,0:T(8,128)(2,1)S(1)}, bf16[5,128,128]{2,1,0:T(8,128)(2,1)}, u32[]{:S(2)}, u32[]{:S(2)}) %collective-permute-start.4) | collective-permute-done | bytes 163872 | tf_op jit(solution)/shard_map/ppermute | solution.py:330
  60.2 8.6 %collective-permute-done.5.refs_6_ = bf16[5,128,128]{2,1,0:T(8,128)(2,1)} collective-permute-done((bf16[5,128,128]{2,1,0:T(8,128)(2,1)S(1)}, bf16[5,128,128]{2,1,0:T(8,128)(2,1)}, u32[]{:S(2)}, u32[]{:S(2)}) %collective-permute-start.5) | collective-permute-done | bytes 163872 | tf_op jit(solution)/shard_map/ppermute | solution.py:330
  68.9 1.8 %collective-permute-done.6.refs_7_ = bf16[5,128,128]{2,1,0:T(8,128)(2,1)} collective-permute-done((bf16[5,128,128]{2,1,0:T(8,128)(2,1)S(1)}, bf16[5,128,128]{2,1,0:T(8,128)(2,1)}, u32[]{:S(2)}, u32[]{:S(2)}) %collective-permute-start.6) | collective-permute-done | bytes 163872 | tf_op jit(solution)/shard_map/ppermute | solution.py:330
  70.7 4.1 %shard_map.88 = (bf16[2,128,128]{2,1,0:T(8,128)(2,1)S(1)}, bf16[2,128,128]{2,1,0:T(8,128)(2,1)S(1)}, bf16[2,128,128]{2,1,0:T(8,128)(2,1)S(1)}, bf16[2,128,128]{2,1,0:T(8,128)(2,1)S(1)}) custom-call(s32[1]{0:T(128)S(6)} %copy.9.first_ref, s32[3,8]{1,0:T(4,128)S(1)} %add_add_fusion.clip_ref, s32[3]{0:T(128)S(1)} %pad_add_fusion.where_ref, ...), custom_call_target="tpu_custom_call" | custom-call | flops 1073741824 | bytes 1835008 | tf_op jit(solution)/shard_map/pallas_call | solution.py:287
  74.8 0.0 copy-start.1
  74.8 0.6 copy-done.1
  75.4 0.0 copy-start.2
  75.4 0.6 copy-done.2
  76.1 0.0 copy-start.3
  76.1 0.6 copy-done.3
  76.7 8.9 %all-to-all-done.x = bf16[8,10,128,128]{3,2,1,0:T(8,128)(2,1)S(1)} async-done(((bf16[8,10,128,128]{3,2,1,0:T(8,128)(2,1)}), bf16[8,10,128,128]{3,2,1,0:T(8,128)(2,1)S(1)}, u32[]{:S(2)}, u32[]{:S(2)}) %all-to-all-start) | async-done | bytes 2621472 | tf_op jit(solution)/shard_map/all_to_all | solution.py:337
  85.6 0.0 collective-permute-start.7
  85.6 2.8 %collective-permute-start.8 = (bf16[2,128,128]{2,1,0:T(8,128)(2,1)}, bf16[2,128,128]{2,1,0:T(8,128)(2,1)S(1)}, u32[]{:S(2)}, u32[]{:S(2)}) collective-permute-start(bf16[2,128,128]{2,1,0:T(8,128)(2,1)} %copy-done.2), channel_id=1, source_target_pairs={{0,16},{4,20},{8,24},{12,28},{16,0},{20,4},{24,8},{28,12},{1,17},{... | collective-permute-start | bytes 196616 | tf_op jit(solution)/shard_map/ppermute | solution.py:330
  88.4 1.5 %collective-permute-start.9 = (bf16[2,128,128]{2,1,0:T(8,128)(2,1)}, bf16[2,128,128]{2,1,0:T(8,128)(2,1)S(1)}, u32[]{:S(2)}, u32[]{:S(2)}) collective-permute-start(bf16[2,128,128]{2,1,0:T(8,128)(2,1)} %copy-done.1), channel_id=1, source_target_pairs={{0,24},{4,28},{8,16},{12,20},{16,8},{20,12},{24,0},{28,4},{1,25},{... | collective-permute-start | bytes 196616 | tf_op jit(solution)/shard_map/ppermute | solution.py:330
  90.0 7.4 %shard_map.89 = (bf16[4,128,128]{2,1,0:T(8,128)(2,1)S(1)}, bf16[4,128,128]{2,1,0:T(8,128)(2,1)S(1)}, bf16[4,128,128]{2,1,0:T(8,128)(2,1)S(1)}, bf16[4,128,128]{2...) custom-call(s32[1]{0:T(128)S(6)} %copy.9.first_ref, ...), custom_call_target="tpu_custom_call" | custom-call | flops 2147483648 | bytes 3670016 | tf_op jit(solution)/shard_map/pallas_call | solution.py:230
  97.4 0.0 collective-permute-done.7.refs_9_
  97.4 0.0 collective-permute-done.8.refs_10_
  97.4 0.0 collective-permute-done.9.refs_11_
  97.4 1.5 %collective-permute-start.10 = (bf16[4,128,128]{2,1,0:T(8,128)(2,1)S(1)}, bf16[4,128,128]{2,1,0:T(8,128)(2,1)S(1)}, u32[]{:S(2)}, u32[]{:S(2)}) collective-permute-start(bf16[4,128,128]{2,1,0:T(8,128)(2,1)S(1)} %get-tuple-element.67), channel_id=1, source_target_pairs={{0,4},{4,0},{8,12},{12,8},{16,20},{20,16},{24,28},{28,24},{1,5},{5... | collective-permute-start | bytes 393224 | tf_op jit(solution)/shard_map/ppermute | solution.py:330
  98.9 0.0 collective-permute-start.11
  98.9 2.0 %collective-permute-start.12 = (bf16[4,128,128]{2,1,0:T(8,128)(2,1)S(1)}, bf16[4,128,128]{2,1,0:T(8,128)(2,1)S(1)}, u32[]{:S(2)}, u32[]{:S(2)}) collective-permute-start(bf16[4,128,128]{2,1,0:T(8,128)(2,1)S(1)} %get-tuple-element.69), channel_id=1, source_target_pairs={{0,12},{4,8},{8,4},{12,0},{16,28},{20,24},{24,20},{28,16},{1,13},{... | collective-permute-start | bytes 393224 | tf_op jit(solution)/shard_map/ppermute | solution.py:330
  101.0 0.8 collective-permute-start.13
  101.8 3.0 %collective-permute-start.14 = (bf16[4,128,128]{2,1,0:T(8,128)(2,1)S(1)}, bf16[4,128,128]{2,1,0:T(8,128)(2,1)S(1)}, u32[]{:S(2)}, u32[]{:S(2)}) collective-permute-start(bf16[4,128,128]{2,1,0:T(8,128)(2,1)S(1)} %get-tuple-element.71), channel_id=1, source_target_pairs={{0,20},{4,16},{8,28},{12,24},{16,4},{20,0},{24,12},{28,8},{1,21},{... | collective-permute-start | bytes 393224 | tf_op jit(solution)/shard_map/ppermute | solution.py:330
  104.8 0.0 collective-permute-done.10.refs_1_
  104.8 1.5 %collective-permute-start.15 = (bf16[4,128,128]{2,1,0:T(8,128)(2,1)S(1)}, bf16[4,128,128]{2,1,0:T(8,128)(2,1)S(1)}, u32[]{:S(2)}, u32[]{:S(2)}) collective-permute-start(bf16[4,128,128]{2,1,0:T(8,128)(2,1)S(1)} %get-tuple-element.72), channel_id=1, source_target_pairs={{0,24},{4,28},{8,16},{12,20},{16,8},{20,12},{24,0},{28,4},{1,25},{... | collective-permute-start | bytes 393224 | tf_op jit(solution)/shard_map/ppermute | solution.py:330
  106.3 0.5 collective-permute-done.11.refs_2_
  106.8 2.7 %collective-permute-start.16 = (bf16[4,128,128]{2,1,0:T(8,128)(2,1)S(1)}, bf16[4,128,128]{2,1,0:T(8,128)(2,1)S(1)}, u32[]{:S(2)}, u32[]{:S(2)}) collective-permute-start(bf16[4,128,128]{2,1,0:T(8,128)(2,1)S(1)} %get-tuple-element.73), channel_id=1, source_target_pairs={{0,28},{4,24},{8,20},{12,16},{16,12},{20,8},{24,4},{28,0},{1,29},{... | collective-permute-start | bytes 393224 | tf_op jit(solution)/shard_map/ppermute | solution.py:330
  109.5 0.0 collective-permute-done.12.refs_3_
  109.5 9.7 %collective-permute-done.13.refs_4_ = bf16[4,128,128]{2,1,0:T(8,128)(2,1)S(1)} collective-permute-done((bf16[4,128,128]{2,1,0:T(8,128)(2,1)S(1)}, bf16[4,128,128]{2,1,0:T(8,128)(2,1)S(1)}, u32[]{:S(2)}, u32[]{:S(2)}) %collective-permute-start.13) | collective-permute-done | bytes 131104 | tf_op jit(solution)/shard_map/ppermute | solution.py:330
  119.2 3.5 %collective-permute-done.14.refs_5_ = bf16[4,128,128]{2,1,0:T(8,128)(2,1)S(1)} collective-permute-done((bf16[4,128,128]{2,1,0:T(8,128)(2,1)S(1)}, bf16[4,128,128]{2,1,0:T(8,128)(2,1)S(1)}, u32[]{:S(2)}, u32[]{:S(2)}) %collective-permute-start.14) | collective-permute-done | bytes 131104 | tf_op jit(solution)/shard_map/ppermute | solution.py:330
  122.6 0.0 collective-permute-done.15.refs_6_
  122.6 0.0 collective-permute-done.16.refs_7_
  122.7 1.8 %shard_map.90 = (bf16[1,128,2560]{2,1,0:T(8,128)(2,1)}, bf16[1,128,2560]{2,1,0:T(8,128)(2,1)}) custom-call(s32[3]{0:T(128)S(1)} %pad_add_fusion.where_ref, bf16[4,128,128]{2,1,0:T(8,128)(2,1)S(1)} %get-tuple-element.66.refs_0_, bf16[4,128,128]{2,1,0:T(8,128)(2,1)S(1)} %collective-permute-done.10.refs_1_, ...), custom_call_target="tpu_custom_call" | custom-call | bytes 2621440 | tf_op jit(solution)/shard_map/pallas_call | solution.py:315
Async XLA Ops:
  2.7 10.0 %collective-permute-start = (bf16[5,128,128]{2,1,0:T(8,128)(2,1)}, bf16[5,128,128]{2,1,0:T(8,128)(2,1)S(1)}, u32[]{:S(2)}, u32[]{:S(2)}) collective-permute-start(bf16[5,128,128]{2,1,0:T(8,128)(2,1)} %get-tuple-element.41), channel_id=1, source_target_pairs={{0,8},{4,12},{8,0},{12,4},{16,24},{20,28},{24,16},{28,20},{1,9},{5... | collective-permute-start | bytes 491528 | tf_op jit(solution)/shard_map/ppermute | solution.py:330
  5.8 15.3 %collective-permute-start.1 = (bf16[5,128,128]{2,1,0:T(8,128)(2,1)}, bf16[5,128,128]{2,1,0:T(8,128)(2,1)S(1)}, u32[]{:S(2)}, u32[]{:S(2)}) collective-permute-start(bf16[5,128,128]{2,1,0:T(8,128)(2,1)} %get-tuple-element.42), channel_id=1, source_target_pairs={{0,16},{4,20},{8,24},{12,28},{16,0},{20,4},{24,8},{28,12},{1,17},{... | collective-permute-start | bytes 491528 | tf_op jit(solution)/shard_map/ppermute | solution.py:330
  8.4 12.7 %collective-permute-start.2 = (bf16[5,128,128]{2,1,0:T(8,128)(2,1)}, bf16[5,128,128]{2,1,0:T(8,128)(2,1)S(1)}, u32[]{:S(2)}, u32[]{:S(2)}) collective-permute-start(bf16[5,128,128]{2,1,0:T(8,128)(2,1)} %get-tuple-element.43), channel_id=1, source_target_pairs={{0,24},{4,28},{8,16},{12,20},{16,8},{20,12},{24,0},{28,4},{1,25},{... | collective-permute-start | bytes 491528 | tf_op jit(solution)/shard_map/ppermute | solution.py:330
  21.1 6.0 %copy-start.4 = (s32[1,3]{1,0:T(1,128)S(1)}, s32[1,3]{1,0:T(1,128)}, u32[]{:S(2)}) copy-start(s32[1,3]{1,0:T(1,128)} %param.13) | copy-start | bytes 40
  21.1 7.6 %copy-start = (bf16[5,128,128]{2,1,0:T(8,128)(2,1)S(1)}, bf16[5,128,128]{2,1,0:T(8,128)(2,1)}, u32[]{:S(2)}) copy-start(bf16[5,128,128]{2,1,0:T(8,128)(2,1)} %get-tuple-element.45.refs_0_) | copy-start | bytes 491524
  21.1 64.5 %all-to-all-start = ((bf16[8,10,128,128]{3,2,1,0:T(8,128)(2,1)}), bf16[8,10,128,128]{3,2,1,0:T(8,128)(2,1)S(1)}, u32[]{:S(2)}, u32[]{:S(2)}) async-start(bf16[8,10,128,128]{3,2,1,0:T(8,128)(2,1)} %shard_map.86), calls=%async_computation | async-start | bytes 5242880 | tf_op jit(solution)/shard_map/all_to_all | solution.py:337
  28.7 25.2 %collective-permute-start.3 = (bf16[5,128,128]{2,1,0:T(8,128)(2,1)S(1)}, bf16[5,128,128]{2,1,0:T(8,128)(2,1)S(1)}, u32[]{:S(2)}, u32[]{:S(2)}) collective-permute-start(bf16[5,128,128]{2,1,0:T(8,128)(2,1)S(1)} %copy-done), channel_id=1, source_target_pairs={{0,4},{4,0},{8,12},{12,8},{16,20},{20,16},{24,28},{28,24},{1,5},{5... | collective-permute-start | bytes 491528 | tf_op jit(solution)/shard_map/ppermute | solution.py:330
  30.8 29.4 %collective-permute-start.4 = (bf16[5,128,128]{2,1,0:T(8,128)(2,1)S(1)}, bf16[5,128,128]{2,1,0:T(8,128)(2,1)}, u32[]{:S(2)}, u32[]{:S(2)}) collective-permute-start(bf16[5,128,128]{2,1,0:T(8,128)(2,1)S(1)} %collective-permute-done.refs_1_), channel_id=1, source_target_pairs={{0,4},{4,0},{8,12},{12,8},{16,20},{20,16},{24,28},{28,24},{1,5},{5... | collective-permute-start | bytes 491528 | tf_op jit(solution)/shard_map/ppermute | solution.py:330
  30.9 38.0 %collective-permute-start.5 = (bf16[5,128,128]{2,1,0:T(8,128)(2,1)S(1)}, bf16[5,128,128]{2,1,0:T(8,128)(2,1)}, u32[]{:S(2)}, u32[]{:S(2)}) collective-permute-start(bf16[5,128,128]{2,1,0:T(8,128)(2,1)S(1)} %collective-permute-done.1.refs_2_), channel_id=1, source_target_pairs={{0,4},{4,0},{8,12},{12,8},{16,20},{20,16},{24,28},{28,24},{1,5},{5... | collective-permute-start | bytes 491528 | tf_op jit(solution)/shard_map/ppermute | solution.py:330
  32.8 37.9 %collective-permute-start.6 = (bf16[5,128,128]{2,1,0:T(8,128)(2,1)S(1)}, bf16[5,128,128]{2,1,0:T(8,128)(2,1)}, u32[]{:S(2)}, u32[]{:S(2)}) collective-permute-start(bf16[5,128,128]{2,1,0:T(8,128)(2,1)S(1)} %collective-permute-done.2.refs_3_), channel_id=1, source_target_pairs={{0,4},{4,0},{8,12},{12,8},{16,20},{20,16},{24,28},{28,24},{1,5},{5... | collective-permute-start | bytes 491528 | tf_op jit(solution)/shard_map/ppermute | solution.py:330
  74.8 0.6 copy-start.1
  75.4 0.6 copy-start.2
  76.1 0.6 copy-start.3
  85.6 11.8 %collective-permute-start.7 = (bf16[2,128,128]{2,1,0:T(8,128)(2,1)}, bf16[2,128,128]{2,1,0:T(8,128)(2,1)S(1)}, u32[]{:S(2)}, u32[]{:S(2)}) collective-permute-start(bf16[2,128,128]{2,1,0:T(8,128)(2,1)} %copy-done.3), channel_id=1, source_target_pairs={{0,8},{4,12},{8,0},{12,4},{16,24},{20,28},{24,16},{28,20},{1,9},{5... | collective-permute-start | bytes 196616 | tf_op jit(solution)/shard_map/ppermute | solution.py:330
  85.6 11.8 %collective-permute-start.8 = (bf16[2,128,128]{2,1,0:T(8,128)(2,1)}, bf16[2,128,128]{2,1,0:T(8,128)(2,1)S(1)}, u32[]{:S(2)}, u32[]{:S(2)}) collective-permute-start(bf16[2,128,128]{2,1,0:T(8,128)(2,1)} %copy-done.2), channel_id=1, source_target_pairs={{0,16},{4,20},{8,24},{12,28},{16,0},{20,4},{24,8},{28,12},{1,17},{... | collective-permute-start | bytes 196616 | tf_op jit(solution)/shard_map/ppermute | solution.py:330
  88.4 9.0 %collective-permute-start.9 = (bf16[2,128,128]{2,1,0:T(8,128)(2,1)}, bf16[2,128,128]{2,1,0:T(8,128)(2,1)S(1)}, u32[]{:S(2)}, u32[]{:S(2)}) collective-permute-start(bf16[2,128,128]{2,1,0:T(8,128)(2,1)} %copy-done.1), channel_id=1, source_target_pairs={{0,24},{4,28},{8,16},{12,20},{16,8},{20,12},{24,0},{28,4},{1,25},{... | collective-permute-start | bytes 196616 | tf_op jit(solution)/shard_map/ppermute | solution.py:330
  97.4 7.4 %collective-permute-start.10 = (bf16[4,128,128]{2,1,0:T(8,128)(2,1)S(1)}, bf16[4,128,128]{2,1,0:T(8,128)(2,1)S(1)}, u32[]{:S(2)}, u32[]{:S(2)}) collective-permute-start(bf16[4,128,128]{2,1,0:T(8,128)(2,1)S(1)} %get-tuple-element.67), channel_id=1, source_target_pairs={{0,4},{4,0},{8,12},{12,8},{16,20},{20,16},{24,28},{28,24},{1,5},{5... | collective-permute-start | bytes 393224 | tf_op jit(solution)/shard_map/ppermute | solution.py:330
  98.9 7.9 %collective-permute-start.11 = (bf16[4,128,128]{2,1,0:T(8,128)(2,1)S(1)}, bf16[4,128,128]{2,1,0:T(8,128)(2,1)S(1)}, u32[]{:S(2)}, u32[]{:S(2)}) collective-permute-start(bf16[4,128,128]{2,1,0:T(8,128)(2,1)S(1)} %get-tuple-element.68), channel_id=1, source_target_pairs={{0,8},{4,12},{8,0},{12,4},{16,24},{20,28},{24,16},{28,20},{1,9},{5... | collective-permute-start | bytes 393224 | tf_op jit(solution)/shard_map/ppermute | solution.py:330
  98.9 10.5 %collective-permute-start.12 = (bf16[4,128,128]{2,1,0:T(8,128)(2,1)S(1)}, bf16[4,128,128]{2,1,0:T(8,128)(2,1)S(1)}, u32[]{:S(2)}, u32[]{:S(2)}) collective-permute-start(bf16[4,128,128]{2,1,0:T(8,128)(2,1)S(1)} %get-tuple-element.69), channel_id=1, source_target_pairs={{0,12},{4,8},{8,4},{12,0},{16,28},{20,24},{24,20},{28,16},{1,13},{... | collective-permute-start | bytes 393224 | tf_op jit(solution)/shard_map/ppermute | solution.py:330
  101.0 18.2 %collective-permute-start.13 = (bf16[4,128,128]{2,1,0:T(8,128)(2,1)S(1)}, bf16[4,128,128]{2,1,0:T(8,128)(2,1)S(1)}, u32[]{:S(2)}, u32[]{:S(2)}) collective-permute-start(bf16[4,128,128]{2,1,0:T(8,128)(2,1)S(1)} %get-tuple-element.70), channel_id=1, source_target_pairs={{0,16},{4,20},{8,24},{12,28},{16,0},{20,4},{24,8},{28,12},{1,17},{... | collective-permute-start | bytes 393224 | tf_op jit(solution)/shard_map/ppermute | solution.py:330
  101.8 20.9 %collective-permute-start.14 = (bf16[4,128,128]{2,1,0:T(8,128)(2,1)S(1)}, bf16[4,128,128]{2,1,0:T(8,128)(2,1)S(1)}, u32[]{:S(2)}, u32[]{:S(2)}) collective-permute-start(bf16[4,128,128]{2,1,0:T(8,128)(2,1)S(1)} %get-tuple-element.71), channel_id=1, source_target_pairs={{0,20},{4,16},{8,28},{12,24},{16,4},{20,0},{24,12},{28,8},{1,21},{... | collective-permute-start | bytes 393224 | tf_op jit(solution)/shard_map/ppermute | solution.py:330
  104.8 17.9 %collective-permute-start.15 = (bf16[4,128,128]{2,1,0:T(8,128)(2,1)S(1)}, bf16[4,128,128]{2,1,0:T(8,128)(2,1)S(1)}, u32[]{:S(2)}, u32[]{:S(2)}) collective-permute-start(bf16[4,128,128]{2,1,0:T(8,128)(2,1)S(1)} %get-tuple-element.72), channel_id=1, source_target_pairs={{0,24},{4,28},{8,16},{12,20},{16,8},{20,12},{24,0},{28,4},{1,25},{... | collective-permute-start | bytes 393224 | tf_op jit(solution)/shard_map/ppermute | solution.py:330
  106.8 15.9 %collective-permute-start.16 = (bf16[4,128,128]{2,1,0:T(8,128)(2,1)S(1)}, bf16[4,128,128]{2,1,0:T(8,128)(2,1)S(1)}, u32[]{:S(2)}, u32[]{:S(2)}) collective-permute-start(bf16[4,128,128]{2,1,0:T(8,128)(2,1)S(1)} %get-tuple-element.73), channel_id=1, source_target_pairs={{0,28},{4,24},{8,20},{12,16},{16,12},{20,8},{24,4},{28,0},{1,29},{... | collective-permute-start | bytes 393224 | tf_op jit(solution)/shard_map/ppermute | solution.py:330
